TPU v7x, 32 devices: a whole 2x2x4 slice. The times are simulated.
32 devices in a mesh: scen: 8 (over z, core), tile: 4 (over y, x).
Axes of the slice: x: 2, y: 2, z: 4, core: 2. Of those that a mesh axis runs over, the one named last changes fastest.
Arguments:
- inv_factor: bfloat16 [32, 1024, 1024], P(('scen', 'tile'))
- border: bfloat16 [32, 1024, 512], P(('scen', 'tile')), may hold values from -0.1875 to 0.1875
- touched: int32 [32, 4], P(('scen', 'tile')), may hold values from 0 to 127, as said below
- live_count: int32 [32], P(('scen', 'tile')), may hold values from 1 to 4, as said below
- regular: float32 [16384], P('scen'), may hold values from 0.5 to 2
Outputs:
- schur_full: float32 [16384, 16384], P('scen', 'tile')
- panel: float32 [16384, 1024], P(('scen', 'tile'))
Inputs may be any that keep to these rules, and one draw needn't show every extreme that they name: `touched`: the 4 block numbers of one scenario lie in 4 different groups of 32 consecutive block numbers. Slots 0 to live_count - 1 of a scenario are live; some scenario has all 4 slots live.
All inputs are finite; a program needn't handle non-finite values.
Results may differ from a plain program's by a relative error of at most 0.0012.
Values sent between devices are 32-bit elements; how exact they have to be, the bound alone decides.
No kernel may reach another device: no remote copies, remote signals or barrier semaphores. Data moves between devices by JAX's collectives and lax.ppermute only.
A program may use at most 192 MiB of HBM per device.

v0:
```python
import jax
import jax.numpy as jnp
from jax import lax
from jax.sharding import PartitionSpec as P

FIRST = 16384
PANEL = 1024


def from_root(array, axis, root):
    mine = lax.axis_index(axis) == root
    return lax.psum(jnp.where(mine, array, jnp.zeros_like(array)), axis)


def local(inv_factor, border, touched, live_count, regular):
    scen_count = lax.axis_size("scen")
    tile_count = lax.axis_size("tile")
    scen_index = lax.axis_index("scen")
    tile_index = lax.axis_index("tile")
    local_count, order_size, width = border.shape
    slot_count = touched.shape[1]
    block_size = width // slot_count
    block_total = FIRST // block_size
    row_span = block_total // scen_count
    col_span = block_total // tile_count
    scaled = jnp.einsum(
        "sij,sjc->sic", inv_factor, border, preferred_element_type=jnp.float32
    ).astype(jnp.bfloat16)
    scaled = scaled.reshape(local_count, order_size, slot_count, block_size)
    live_mask = jnp.arange(slot_count, dtype=jnp.int32)[None, :] < live_count[:, None]
    row_select = live_mask[:, None, :] & (
        (touched // row_span)[:, None, :] == jnp.arange(scen_count, dtype=jnp.int32)[None, :, None]
    )
    col_select = live_mask[:, None, :] & (
        (touched // col_span)[:, None, :] == jnp.arange(tile_count, dtype=jnp.int32)[None, :, None]
    )
    row_blocks = jnp.einsum(
        "skmb,sgm->skgb",
        scaled,
        row_select.astype(jnp.bfloat16),
        preferred_element_type=jnp.float32,
    ).astype(jnp.bfloat16)
    col_blocks = jnp.einsum(
        "skmb,shm->skhb",
        scaled,
        col_select.astype(jnp.bfloat16),
        preferred_element_type=jnp.float32,
    ).astype(jnp.bfloat16)
    outgoing = jnp.einsum(
        "skgb,skhc->ghsbc", row_blocks, col_blocks, preferred_element_type=jnp.float32
    )
    row_label = jnp.max(jnp.where(row_select, touched[:, None, :], -1), axis=2)
    col_label = jnp.max(jnp.where(col_select, touched[:, None, :], -1), axis=2)
    labels = jnp.stack(
        jnp.broadcast_arrays(row_label.T[:, None, :], col_label.T[None, :, :]), axis=3
    ).astype(jnp.int32)
    halfway, halfway_labels = (
        lax.all_to_all(outgoing, "tile", split_axis=1, concat_axis=1, tiled=True),
        lax.all_to_all(labels, "tile", split_axis=1, concat_axis=1, tiled=True),
    )
    arrived, arrived_labels = (
        lax.all_to_all(halfway, "scen", split_axis=0, concat_axis=0, tiled=True),
        lax.all_to_all(halfway_labels, "scen", split_axis=0, concat_axis=0, tiled=True),
    )
    source_total = arrived.shape[0] * arrived.shape[1] * arrived.shape[2]
    flat_blocks = arrived.reshape(source_total, block_size * block_size)
    flat_labels = arrived_labels.reshape(source_total, 2)
    row_offset = flat_labels[:, 0] - scen_index * row_span
    col_offset = flat_labels[:, 1] - tile_index * col_span
    usable = (flat_labels[:, 0] >= 0) & (flat_labels[:, 1] >= 0)
    slot_total = row_span * col_span
    position = jnp.where(usable, row_offset * col_span + col_offset, slot_total).astype(jnp.int32)
    summed = jax.ops.segment_sum(flat_blocks, position, num_segments=slot_total + 1)[:slot_total]
    tile_sum = summed.reshape(row_span, col_span, block_size, block_size).transpose(0, 2, 1, 3)
    tile_sum = tile_sum.reshape(row_span * block_size, col_span * block_size)
    row_global = scen_index * (row_span * block_size) + jnp.arange(
        row_span * block_size, dtype=jnp.int32
    )
    col_global = tile_index * (col_span * block_size) + jnp.arange(
        col_span * block_size, dtype=jnp.int32
    )
    schur_tile = tile_sum + jnp.where(
        row_global[:, None] == col_global[None, :], regular[:, None], 0.0
    )
    strip_rows = from_root(schur_tile[:, :PANEL], "tile", 0)
    corner = from_root(schur_tile[:PANEL, :PANEL], ("scen", "tile"), 0)
    corner_factor = jnp.linalg.cholesky(corner)
    row_share = strip_rows.shape[0] // tile_count
    own_rows = lax.dynamic_slice_in_dim(strip_rows, tile_index * row_share, row_share, 0)
    panel = lax.linalg.triangular_solve(
        corner_factor, own_rows, left_side=False, lower=True, transpose_a=True
    )
    return (schur_tile, panel)


def solution(mesh):
    return jax.shard_map(
        local,
        mesh=mesh,
        in_specs=(
            P(("scen", "tile"), None, None),
            P(("scen", "tile"), None, None),
            P(("scen", "tile"), None),
            P(("scen", "tile")),
            P("scen"),
        ),
        out_specs=(P("scen", "tile"), P(("scen", "tile"), None)),
        check_vma=False,
    )
```

profile of v0, /device:TPU:0, one launch (start us, length us, event | category | flops | bytes accessed | tf_op | source)
XLA Modules:
  0.0 756.2 jit_solution(14740050704889891334)
XLA Ops:
  10.9 5.2 all-to-all-start
  16.0 2.5 fusion.13
  21.2 2.6 fusion.10
  23.8 4.2 all-to-all-start.2
  28.7 23.6 %all-to-all-done.2 = f32[8,4,1,128,128]{3,4,0,2,1:T(8,128)S(1)} async-done(((f32[8,4,1,128,128]{3,4,0,2,1:T(8,128)}), f32[8,4,1,128,128]{3,4,0,2,1:T(8,128)S(1)}, u32[]{:S(2)}, u32[]{:S(2)}) %all-to-all-start.2) | async-done | bytes 2097184 | tf_op jit(solution)/shard_map/all_to_all | solution.py:58
  52.3 4.9 all-to-all-start.1
  58.7 4.1 all-to-all-done.1
  62.8 4.3 all-to-all-start.3
  67.3 48.9 %all-to-all-done.3 = f32[8,4,1,128,128]{3,4,1,2,0:T(8,128)} async-done(((f32[8,4,1,128,128]{3,4,1,2,0:T(8,128)}), f32[8,4,1,128,128]{3,4,1,2,0:T(8,128)}, u32[]{:S(2)}, u32[]{:S(2)}) %all-to-all-start.3) | async-done | bytes 2097184 | tf_op jit(solution)/shard_map/all_to_all | solution.py:62
  116.2 1.9 copy.99
  118.1 17.9 %scatter_custom_fusion = f32[513,16384]{1,0:T(8,128)} fusion(s32[32]{0:T(128)S(1)} %fusion.89, f32[]{:T(128)} %constant.302.clone.1, f32[4,8,128,128]{3,2,1,0:T(8,128)S(1)} %bitcast.176), kind=kCustom, calls=%fused_computation.6 | custom fusion | flops 524288 | bytes 35717124 | tf_op jit(solution)/shard_map/scatter-add | solution.py:73
  136.0 12.2 %slice_bitcast_fusion = f32[64,8,128,128]{3,1,2,0:T(8,128)S(1)} fusion(f32[513,16384]{1,0:T(8,128)} %scatter_custom_fusion), kind=kLoop, calls=%fused_computation.5 | loop fusion | bytes 67108864
  148.2 12.4 %copy.145 = f32[64,8,128,128]{3,2,1,0:T(8,128)} copy(f32[64,8,128,128]{3,1,2,0:T(8,128)S(1)} %slice_bitcast_fusion) | data formatting | bytes 67108864
  160.6 23.2 %bitcast_bitcast_fusion = f32[16,128,32,128]{3,1,2,0:T(8,128)} fusion(f32[16,32,128,128]{3,2,1,0:T(8,128)} %bitcast.175), kind=kLoop, calls=%fused_computation.4 | loop fusion | bytes 67108864 | tf_op jit(solution)/shard_map/transpose | solution.py:74
  183.8 33.4 %copy.100 = f32[16,128,32,128]{1,0,3,2:T(8,128)} copy(f32[16,128,32,128]{3,1,2,0:T(8,128)} %bitcast_bitcast_fusion) | data formatting | bytes 67108864 | tf_op jit(solution)/shard_map/transpose | solution.py:74
  217.2 23.5 %bitcast_add_fusion = f32[2048,4096]{0,1:T(8,128)S(1)} fusion(f32[512,8,16,128]{3,2,1,0:T(8,128)} %bitcast.174, f32[2048]{0:T(1024)S(1)} %copy-done.4, s32[2048]{0:T(1024)S(1)} %iota_add_fusion.1, s32[4096]{0:T(1024)S(1)} %iota_add_fusion), kind=kLoop, calls=%fused_computation.3 | loop fusion | flops 25165824 | bytes 67141632 | tf_op jit(solution)/shard_map/add | solution.py:82
  240.7 11.1 %copy-done.2 = f32[2048,4096]{0,1:T(8,128)} copy-done((f32[2048,4096]{0,1:T(8,128)}, f32[2048,4096]{0,1:T(8,128)S(1)}, u32[]{:S(2)}) %copy-start.2) | copy-done | bytes 33554456
  251.7 2.4 slice_select_fusion.1
  254.2 31.3 %copy.125 = f32[2048,4096]{1,0:T(8,128)} copy(f32[2048,4096]{0,1:T(8,128)} %copy-done.2) | data formatting | bytes 67108864
  285.5 8.2 %slice_select_fusion = f32[2048,1024]{0,1:T(8,128)} fusion(f32[2048,4096]{0,1:T(8,128)} %copy-done.2, pred[]{:T(512)S(6)} %eq.100), kind=kLoop, calls=%fused_computation.8 | loop fusion | flops 2097152 | bytes 16777216 | tf_op jit(solution)/shard_map/jit(_where)/select_n | solution.py:12
  293.8 100.2 %all-reduce.6.cloned.1.call-done = f32[1024,1024]{0,1:T(8,128)} async-done(((f32[1024,1024]{0,1:T(8,128)}), f32[1024,1024]{0,1:T(8,128)}) %all-reduce.6.cloned.1.call-update) | async-done | bytes 4194320 | tf_op jit(solution)/shard_map/psum | solution.py:12
  394.0 5.5 copy.101
  399.5 5.4 fusion.2
  404.9 2.0 copy-done.3
  406.9 11.7 %cholesky.222 = f32[128,128]{1,0:T(8,128)S(1)} custom-call(f32[128,128]{1,0:T(8,128)S(1)} %cholesky.577), custom_call_target="Cholesky" | custom-call | tf_op jit(solution)/shard_map/jit(cholesky)/cholesky | solution.py:87
  418.6 9.8 %custom-call.62 = f32[1,128,128]{1,2,0:T(8,128)S(1)} custom-call(f32[1,128,128]{2,1,0:T(8,128)S(1)} %get-tuple-element.82), custom_call_target="InvertDiagBlocksLowerTriangular" | custom-call | tf_op jit(solution)/shard_map/jit(cholesky)/cholesky | solution.py:87
  431.6 11.7 %cholesky.243 = f32[128,128]{1,0:T(8,128)S(1)} custom-call(f32[128,128]{1,0:T(8,128)S(1)} %cholesky.581), custom_call_target="Cholesky" | custom-call | tf_op jit(solution)/shard_map/jit(cholesky)/cholesky | solution.py:87
  443.9 2.5 cholesky.254
  446.4 9.8 %custom-call.63 = f32[1,128,128]{1,2,0:T(8,128)S(1)} custom-call(f32[1,128,128]{2,1,0:T(8,128)S(1)} %get-tuple-element.80), custom_call_target="InvertDiagBlocksLowerTriangular" | custom-call | tf_op jit(solution)/shard_map/jit(cholesky)/cholesky | solution.py:87
  459.0 2.7 convolution_subtract_fusion.1
  461.7 11.7 %cholesky.466 = f32[128,128]{1,0:T(8,128)S(1)} custom-call(f32[128,128]{1,0:T(8,128)S(1)} %cholesky.586), custom_call_target="Cholesky" | custom-call | tf_op jit(solution)/shard_map/jit(cholesky)/cholesky | solution.py:87
  474.2 9.8 %custom-call.64 = f32[1,128,128]{1,2,0:T(8,128)S(1)} custom-call(f32[1,128,128]{2,1,0:T(8,128)S(1)} %get-tuple-element.78), custom_call_target="InvertDiagBlocksLowerTriangular" | custom-call | tf_op jit(solution)/shard_map/jit(cholesky)/cholesky | solution.py:87
  485.3 3.5 convolution_subtract_fusion.2
  488.8 11.7 %cholesky.485 = f32[128,128]{1,0:T(8,128)S(1)} custom-call(f32[128,128]{1,0:T(8,128)S(1)} %cholesky.591), custom_call_target="Cholesky" | custom-call | tf_op jit(solution)/shard_map/jit(cholesky)/cholesky | solution.py:87
  500.7 9.8 %custom-call.65 = f32[1,128,128]{1,2,0:T(8,128)S(1)} custom-call(f32[1,128,128]{2,1,0:T(8,128)S(1)} %get-tuple-element.76), custom_call_target="InvertDiagBlocksLowerTriangular" | custom-call | tf_op jit(solution)/shard_map/jit(cholesky)/cholesky | solution.py:87
  512.2 3.2 convolution_subtract_fusion.10
  515.4 11.8 %cholesky.504 = f32[128,128]{1,0:T(8,128)S(1)} custom-call(f32[128,128]{1,0:T(8,128)S(1)} %cholesky.596), custom_call_target="Cholesky" | custom-call | tf_op jit(solution)/shard_map/jit(cholesky)/cholesky | solution.py:87
  527.4 9.8 %custom-call.66 = f32[1,128,128]{1,2,0:T(8,128)S(1)} custom-call(f32[1,128,128]{2,1,0:T(8,128)S(1)} %get-tuple-element.74), custom_call_target="InvertDiagBlocksLowerTriangular" | custom-call | tf_op jit(solution)/shard_map/jit(cholesky)/cholesky | solution.py:87
  539.0 3.1 convolution_subtract_fusion.11
  542.1 11.7 %cholesky.524 = f32[128,128]{1,0:T(8,128)S(1)} custom-call(f32[128,128]{1,0:T(8,128)S(1)} %cholesky.601), custom_call_target="Cholesky" | custom-call | tf_op jit(solution)/shard_map/jit(cholesky)/cholesky | solution.py:87
  554.0 9.8 %custom-call.67 = f32[1,128,128]{1,2,0:T(8,128)S(1)} custom-call(f32[1,128,128]{2,1,0:T(8,128)S(1)} %get-tuple-element.72), custom_call_target="InvertDiagBlocksLowerTriangular" | custom-call | tf_op jit(solution)/shard_map/jit(cholesky)/cholesky | solution.py:87
  565.4 2.9 convolution_subtract_fusion.12
  568.3 11.7 %cholesky.544 = f32[128,128]{1,0:T(8,128)S(1)} custom-call(f32[128,128]{1,0:T(8,128)S(1)} %cholesky.606), custom_call_target="Cholesky" | custom-call | tf_op jit(solution)/shard_map/jit(cholesky)/cholesky | solution.py:87
  580.1 9.8 %custom-call.68 = f32[1,128,128]{1,2,0:T(8,128)S(1)} custom-call(f32[1,128,128]{2,1,0:T(8,128)S(1)} %get-tuple-element.70), custom_call_target="InvertDiagBlocksLowerTriangular" | custom-call | tf_op jit(solution)/shard_map/jit(cholesky)/cholesky | solution.py:87
  591.5 2.1 convolution_subtract_fusion.13
  593.6 11.7 %cholesky.562 = f32[128,128]{1,0:T(8,128)S(1)} custom-call(f32[128,128]{1,0:T(8,128)S(1)} %convolution_subtract_fusion.13), custom_call_target="Cholesky" | custom-call | tf_op jit(solution)/shard_map/jit(cholesky)/cholesky | solution.py:87
  615.7 4.9 select_select_fusion
  620.6 23.3 %while.1 = (s32[]{:T(128)}, f32[1024,1024]{0,1:T(8,128)}, s32[8,2]{0,1:T(2,128)S(1)}, f32[8,128,128]{2,1,0:T(8,128)S(1)}, s32[]{:T(128)}) while((s32[]{:T(128)}, f32[1024,1024]{0,1:T(8,128)}, s32[8,2]{0,1:T(2,128)S(1)}, f32[8,128,128]{2,1,0:T(8,128)S(1)}, s32[]{:T(128)}) %tuple.62), condition=%wide.while_cond, body=%wide.while_body.sunk | while | flops 2 | bytes 393321 | solution.py:90
  621.2 2.2 dynamic-slice.26
  624.1 2.2 dynamic-slice.26
  627.0 2.2 dynamic-slice.26
  629.9 2.2 dynamic-slice.26
  632.9 2.2 dynamic-slice.26
  635.8 2.2 dynamic-slice.26
  638.7 2.2 dynamic-slice.26
  641.6 2.1 dynamic-slice.26
  643.9 78.8 %custom-call.69 = f32[8,128,128]{1,2,0:T(8,128)S(1)} custom-call(f32[8,128,128]{2,1,0:T(8,128)S(1)} %get-tuple-element.9), custom_call_target="InvertDiagBlocksLowerTriangular" | custom-call | tf_op jit(solution)/shard_map/triangular_solve | solution.py:90
  722.8 2.1 constant_dynamic-update-slice_fusion.17
  730.2 1.7 convolution_subtract_fusion.8
  733.1 1.8 convolution_subtract_fusion.9
  736.1 2.0 convolution_subtract_fusion.4
  739.2 2.2 convolution_subtract_fusion.7
  742.6 2.4 convolution_subtract_fusion.3
  746.1 2.9 copy.126
  (122 shorter events, 45.6 us)
Async XLA Ops:
  7.2 8.9 %copy-start = (bf16[1,1024,1024]{2,1,0:T(8,128)(2,1)S(1)}, bf16[1,1024,1024]{2,1,0:T(8,128)(2,1)}, u32[]{:S(2)}) copy-start(bf16[1,1024,1024]{2,1,0:T(8,128)(2,1)} %param.5) | copy-start | bytes 6291460
  10.9 13.0 %all-to-all-start = ((s32[8,4,1,2]{0,3,2,1:T(2,128)}), s32[8,4,1,2]{0,3,2,1:T(2,128)S(1)}, u32[]{:S(2)}, u32[]{:S(2)}) async-start(s32[8,4,1,2]{0,3,2,1:T(2,128)} %pad_add_fusion), calls=%async_computation | async-start | bytes 8192 | tf_op jit(solution)/shard_map/all_to_all | solution.py:59
  23.8 28.5 %all-to-all-start.2 = ((f32[8,4,1,128,128]{3,4,0,2,1:T(8,128)}), f32[8,4,1,128,128]{3,4,0,2,1:T(8,128)S(1)}, u32[]{:S(2)}, u32[]{:S(2)}) async-start(f32[8,4,1,128,128]{3,4,0,2,1:T(8,128)} %fusion.10), calls=%async_computation.2 | async-start | bytes 4194304 | tf_op jit(solution)/shard_map/all_to_all | solution.py:58
  52.3 10.5 %all-to-all-start.1 = ((s32[8,4,1,2]{1,3,2,0:T(2,128)}), s32[8,4,1,2]{1,3,2,0:T(2,128)S(1)}, u32[]{:S(2)}, u32[]{:S(2)}) async-start(s32[8,4,1,2]{1,3,2,0:T(2,128)} %copy.91), calls=%async_computation.1 | async-start | bytes 16384 | tf_op jit(solution)/shard_map/all_to_all | solution.py:63
  62.8 53.4 %all-to-all-start.3 = ((f32[8,4,1,128,128]{3,4,1,2,0:T(8,128)}), f32[8,4,1,128,128]{3,4,1,2,0:T(8,128)}, u32[]{:S(2)}, u32[]{:S(2)}) async-start(f32[8,4,1,128,128]{3,4,1,2,0:T(8,128)} %copy.98), calls=%async_computation.3 | async-start | bytes 4194304 | tf_op jit(solution)/shard_map/all_to_all | solution.py:62
  67.1 326.9 %all-reduce.6.cloned.1.call-start = ((), (), s32[]{:S(2)}) async-start(), calls=%async_computation.5 | async-start | bytes 8388608 | tf_op jit(solution)/shard_map/psum | solution.py:12
  183.8 33.4 %copy-start.4 = (f32[2048]{0:T(1024)S(1)}, f32[2048]{0:T(1024)}, u32[]{:S(2)}) copy-start(f32[2048]{0:T(1024)} %param.9) | copy-start | bytes 24580
  240.7 11.1 %copy-start.2 = (f32[2048,4096]{0,1:T(8,128)}, f32[2048,4096]{0,1:T(8,128)S(1)}, u32[]{:S(2)}) copy-start(f32[2048,4096]{0,1:T(8,128)S(1)} %bitcast_add_fusion) | copy-start | bytes 100663296
  254.1 468.6 %all-reduce.4.cloned.1.call-start = ((), (), s32[]{:S(2)}) async-start(), calls=%async_computation.4 | async-start | bytes 16777216 | tf_op jit(solution)/shard_map/psum | solution.py:12
  404.9 2.0 copy-start.3
  741.4 7.5 copy-start.1
Sparse Core Ops, SparseCore 0:
  254.3 139.7 all-reduce.5
  397.6 171.0 all-reduce.3
where the time goes:
time: 766 us; the launch traced here: 756 us
  other arithmetic  311 us (41%)
  waiting for transfers between devices  177 us (23%)
  local copies, waits for them, and re-layouts  171 us (22%)
  matrix products  57.5 us (8%)
  between operations  20.9 us (3%)
  starting transfers between devices  18.7 us (2%)
    another operation x30, other arithmetic, local(): corner_factor = jnp.linalg.cholesky(corner)  167 us
    psum x2, waiting for transfers between devices, from_root(): return lax.psum(jnp.where(mine, array, jnp.zeros_like(array)), axis)  100 us
    another operation x3, other arithmetic, local(): lax.linalg.triangular_solve(corner_factor, own_rows, left_side=False, low...  83.7 us
    unnamed x14, local copies, waits for them, and re-layouts  71.8 us
    transpose x2, local copies, waits for them, and re-layouts, local(): summed.reshape(row_span, col_span, block_size, block_size)  56.6 us
    all_to_all x1, waiting for transfers between devices, local(): lax.all_to_all(halfway, 'scen', split_axis=0, concat_axis=0, tiled=True)  48.9 us
    another operation x14, matrix products, local(): corner_factor = jnp.linalg.cholesky(corner)  27.2 us
    another operation x41, local copies, waits for them, and re-layouts  23.8 us
  transfers between devices with their start and end apart: 6, of which 4 were waited for; matrix products, arithmetic and copies ran while one was open for 49% of the time, Pallas kernels for 0%

commit v1 on v0

v1 whole, which is shorter than its diff:
```python
import functools

import jax
import jax.numpy as jnp
from jax import lax
from jax.experimental import pallas as pl
from jax.experimental.pallas import tpu as pltpu
from jax.sharding import PartitionSpec as P

FIRST = 16384
PANEL = 1024
STEPS = 4
PIVOTS = 8
MIB = 1 << 20

SMEM = pl.BlockSpec(memory_space=pltpu.SMEM)
VMEM = pl.BlockSpec(memory_space=pltpu.VMEM)
ANY = pl.BlockSpec(memory_space=pl.ANY)


def gram_kernel(
    groups, block, group_size, ratio, touched_ref, live_ref, regular_ref, inv_ref, border_ref,
    main_ref, panel_ref, corner_ref, border_scr, scaled_scr,
):
    step = pl.program_id(0)
    rows = inv_ref.shape[0]

    def slot_of(group):
        slot = jnp.int32(0)
        for m in range(groups):
            slot = jnp.where(touched_ref[0, m] // group_size == group, m, slot)
        return slot

    @pl.when(step == 0)
    def order_slots():
        for group in range(groups):
            slot = slot_of(group)
            columns = border_ref[:, pl.ds(pl.multiple_of(slot * block, block), block)]
            keep = (slot < live_ref[0]).astype(jnp.float32)
            border_scr[:, group * block:(group + 1) * block] = columns * keep.astype(columns.dtype)

    scaled = jnp.dot(inv_ref[...], border_scr[...], preferred_element_type=jnp.float32)
    scaled_scr[pl.ds(pl.multiple_of(step * rows, rows), rows), :] = scaled.astype(scaled_scr.dtype)

    @pl.when(step == pl.num_programs(0) - 1)
    def finish():
        for group in range(groups):
            strip = lax.dot_general(
                scaled_scr[:, group * block:(group + 1) * block],
                scaled_scr[...],
                (((0,), (0,)), ((), ())),
                preferred_element_type=jnp.float32,
            )
            for other in range(groups):
                main_ref[group * groups + other] = strip[:, other * block:(other + 1) * block]
        place = lax.axis_index("scen") // ratio
        for k in range(groups):
            panel_ref[k] = main_ref[(place ^ k) * groups]
        corner_ref[:block, :] = main_ref[0]
        is_root = (lax.axis_index("scen") == 0) & (lax.axis_index("tile") == 0)
        batch = corner_ref.shape[0] - block - 8
        corner_ref[block:block + batch, :] = regular_ref[:batch, :] * is_root.astype(jnp.float32)
        lane = lax.broadcasted_iota(jnp.int32, (8, block), 1)
        labels = jnp.zeros((8, block), jnp.float32)
        for group in range(groups):
            slot = slot_of(group)
            label = jnp.where(slot < live_ref[0], touched_ref[0, slot], -1)
            labels = jnp.where(lane == group, label.astype(jnp.float32), labels)
        corner_ref[block + batch:, :] = labels


def pivot_rows(rows, start, lane):
    count = len(rows)
    block = lane.shape[1]
    entry = {}
    for a in range(count):
        for b in range(a, count):
            entry[a, b] = jnp.broadcast_to(rows[a][:, b:b + 1], lane.shape)
    lower = {}
    for a in range(count):
        lower[a, a] = 1.0 / entry[a, a]
        for b in range(a + 1, count):
            lower[b, a] = entry[a, b] * lower[a, a]
            for c in range(b, count):
                entry[b, c] = entry[b, c] - lower[b, a] * entry[a, c]
    whole, mults, pivots, done = [], [], [], []
    for a in range(count):
        row = rows[a]
        for b in range(a):
            row = jnp.where(lane == b, 0.0, row) - lower[a, b] * whole[b]
        mults.append(row * lower[a, a])
        whole.append(jnp.where(lane == a, 1.0, row))
        pivots.append(jnp.where((lane > a) & (lane < count), 0.0, whole[a]))
        keep = (lane <= a) | (lane >= block - start)
        done.append(jnp.where(keep, whole[a] * lax.rsqrt(entry[a, a]), 0.0))
    return mults, pivots, done


def split_three(value):
    high = value.astype(jnp.bfloat16).astype(jnp.float32)
    rest = value - high
    middle = rest.astype(jnp.bfloat16).astype(jnp.float32)
    return high, middle, rest - middle


def factor_kernel(batch, block, label_ref, *refs):
    *piece_refs, out_ref, sum_scr, mult_scr, pivot_scr = refs
    sum_scr[...] = jnp.zeros_like(sum_scr)
    diagonal = jnp.zeros((batch, block), jnp.float32)
    base = 0
    for piece in piece_refs:
        for i in range(piece.shape[0]):
            diagonal = diagonal + piece[i, block:block + batch, :]

        def add_one(i, unused, piece=piece, base=base):
            label = label_ref[base + i, 0]

            @pl.when((label >= 0) & (label < batch))
            def add():
                at = pl.ds(pl.multiple_of(label * block, block), block)
                sum_scr[at, :] += piece[i, :block, :]

            return unused

        lax.fori_loop(0, piece.shape[0], add_one, 0)
        base += piece.shape[0]
    row_id = lax.broadcasted_iota(jnp.int32, (block, block), 0)
    col_id = lax.broadcasted_iota(jnp.int32, (block, block), 1)
    for j in range(batch):
        at = slice(j * block, (j + 1) * block)
        sum_scr[at, :] += jnp.where(row_id == col_id, diagonal[j:j + 1, :], 0.0)
    lane = lax.broadcasted_iota(jnp.int32, (batch, block), 1)

    def eliminate(turn, unused):
        start = turn * PIVOTS
        rows = [
            pltpu.roll(sum_scr[pl.ds(start + a, batch, stride=block), :], block - start, 1)
            for a in range(PIVOTS)
        ]
        mults, pivots, done = pivot_rows(rows, start, lane)
        below = (lane >= PIVOTS) & (lane < block - start)
        for a in range(PIVOTS):
            at = slice(a * batch, (a + 1) * batch)
            out_ref[pl.ds(start + a, batch, stride=block), :] = pltpu.roll(done[a], start, 1)
            mult_scr[at, :] = pltpu.roll(jnp.where(below, mults[a], 0.0), start, 1)
            pivot_scr[at, :] = pltpu.roll(pivots[a], start, 1)
        pivot_lane = (col_id >= start) & (col_id < start + PIVOTS)
        for j in range(batch):
            high, middle, low = split_three(mult_scr[pl.ds(j, PIVOTS, stride=batch), :])
            left = jnp.concatenate([high, high, middle, high, middle, low])
            high, middle, low = split_three(pivot_scr[pl.ds(j, PIVOTS, stride=batch), :])
            right = jnp.concatenate([high, middle, high, low, middle, high])
            change = lax.dot_general(
                left.astype(jnp.bfloat16), right.astype(jnp.bfloat16),
                (((0,), (0,)), ((), ())), preferred_element_type=jnp.float32,
            )
            at = slice(j * block, (j + 1) * block)
            sum_scr[at, :] = jnp.where(pivot_lane, 0.0, sum_scr[at, :]) - change
        return unused

    lax.fori_loop(0, block // PIVOTS, eliminate, 0)


def split(value):
    high = value.astype(jnp.bfloat16)
    low = (value - high.astype(jnp.float32)).astype(jnp.bfloat16)
    return high, low


def times_transposed(left, right):
    dims = (((1,), (1,)), ((), ()))
    left_high, left_low = split(left)
    right_high, right_low = split(right)
    dot = functools.partial(
        lax.dot_general, dimension_numbers=dims, preferred_element_type=jnp.float32
    )
    return dot(left_high, right_high) + (dot(left_high, right_low) + dot(left_low, right_high))


def panel_kernel(batch, block, ratio, label_ref, regular_ref, inverse_ref, *refs):
    *piece_refs, out_ref, sum_scr = refs
    share = out_ref.shape[0]
    tile_count = lax.axis_size("tile")
    first_row = (lax.axis_index("scen") * tile_count + lax.axis_index("tile")) * share
    place = lax.axis_index("scen") // ratio
    sum_scr[...] = jnp.zeros_like(sum_scr)
    base = 0
    for piece in piece_refs:

        def add_one(i, unused, piece=piece, base=base):
            row = label_ref[base + i, place] * block
            column = label_ref[base + i, 0]
            wanted = (column >= 0) & (column < batch) & (row >= 0)
            if share >= block:
                wanted = wanted & (row >= first_row) & (row < first_row + share)
            else:
                wanted = wanted & (row <= first_row) & (first_row < row + block)

            @pl.when(wanted)
            def add():
                if share >= block:
                    at = pl.multiple_of(row - first_row, block)
                    sum_scr[column, pl.ds(at, block), :] += piece[i]
                else:
                    at = pl.multiple_of(first_row - row, share)
                    sum_scr[column] += piece[i, pl.ds(at, share), :]

            return unused

        lax.fori_loop(0, piece.shape[0], add_one, 0)
        base += piece.shape[0]

    @pl.when(first_row < batch * block)
    def add_diagonal():
        for j in range(batch):
            row_id = first_row + lax.broadcasted_iota(jnp.int32, (share, block), 0)
            col_id = j * block + lax.broadcasted_iota(jnp.int32, (share, block), 1)
            sum_scr[j] += jnp.where(row_id == col_id, regular_ref[j:j + 1, :], 0.0)

    for j in range(batch):
        product = times_transposed(sum_scr[j], inverse_ref[j * block:(j + 1) * block, :])
        out_ref[:, j * block:(j + 1) * block] = product


def scatter_kernel(block, ratio, label_ref, regular_ref, *refs):
    *piece_refs, back_ref, out_ref, sum_scr, owner_ref, spot_ref, sems = refs
    row_id = lax.broadcasted_iota(jnp.int32, (block, block), 0)
    col_id = lax.broadcasted_iota(jnp.int32, (block, block), 1)
    scen, tile = lax.axis_index("scen"), lax.axis_index("tile")
    tile_count = lax.axis_size("tile")
    place = scen // ratio
    tall, wide = out_ref.shape[0] // block, out_ref.shape[1] // block

    def clear(i, unused):
        owner_ref[i] = -1
        return unused

    lax.fori_loop(0, tall * wide, clear, 0)

    def copy(i):
        spot = spot_ref[i]
        row = pl.multiple_of(spot // wide * block, block)
        column = pl.multiple_of(spot % wide * block, block)
        return pltpu.make_async_copy(
            sum_scr.at[i], out_ref.at[pl.ds(row, block), pl.ds(column, block)], sems.at[i]
        )

    base = 0
    for piece in piece_refs:

        def add_one(i, unused, piece=piece, base=base):
            sender = base + ((i % tile_count) ^ tile) * (piece.shape[0] // tile_count) + ((i // tile_count) ^ place)
            row, column = label_ref[sender, place], label_ref[sender, tile]
            inside = (row >= scen * tall) & (row < (scen + 1) * tall) & (column >= 0)
            spot = jnp.where(inside, (row - scen * tall) * wide + column - tile * wide, 0)
            owner = owner_ref[spot]
            spot_ref[base + i] = jnp.where(inside & (owner < 0), spot, -1)

            @pl.when(inside & (owner < 0))
            def put():
                owner_ref[spot] = base + i
                values = regular_ref[pl.ds(spot // wide, 1), :] * (row == column).astype(jnp.float32)
                sum_scr[base + i] = piece[i] + jnp.where(row_id == col_id, values, 0.0)

            @pl.when(inside & (owner >= 0))
            def add():
                sum_scr[owner] += piece[i]

            return unused

        lax.fori_loop(0, piece.shape[0], add_one, 0)
        base += piece.shape[0]

    def start_one(i, unused):
        @pl.when(spot_ref[i] >= 0)
        def start():
            copy(i).start()

        return unused

    def wait_one(i, unused):
        @pl.when(spot_ref[i] >= 0)
        def wait():
            copy(i).wait()

        return unused

    lax.fori_loop(0, base, start_one, 0)
    lax.fori_loop(0, base, wait_one, 0)


def local(inv_factor, border, touched, live_count, regular):
    scen_count = lax.axis_size("scen")
    tile_count = lax.axis_size("tile")
    scen_index = lax.axis_index("scen")
    tile_index = lax.axis_index("tile")
    local_count, order_size, width = border.shape
    groups = touched.shape[1]
    block = width // groups
    block_total = FIRST // block
    group_size = block_total // groups
    batch = PANEL // block
    ratio = scen_count // groups
    row_span = block_total // scen_count
    row_share = FIRST // (scen_count * tile_count)
    assert local_count == 1 and tile_count == groups and scen_count == groups * ratio
    assert batch <= group_size and batch * block <= regular.shape[0]
    both = ("scen", "tile")
    regular_rows = regular.reshape(-1, block)

    main, strip, corner = pl.pallas_call(
        functools.partial(gram_kernel, groups, block, group_size, ratio),
        grid=(STEPS,),
        in_specs=[
            SMEM, SMEM,
            pl.BlockSpec(regular_rows.shape, lambda i: (0, 0)),
            pl.BlockSpec((order_size // STEPS, order_size), lambda i: (i, 0)),
            pl.BlockSpec((order_size, width), lambda i: (0, 0)),
        ],
        out_specs=[
            pl.BlockSpec((groups * groups, block, block), lambda i: (0, 0, 0)),
            pl.BlockSpec((groups, block, block), lambda i: (0, 0, 0)),
            pl.BlockSpec((block + batch + 8, block), lambda i: (0, 0)),
        ],
        out_shape=[
            jax.ShapeDtypeStruct((groups * groups, block, block), jnp.float32),
            jax.ShapeDtypeStruct((groups, block, block), jnp.float32),
            jax.ShapeDtypeStruct((block + batch + 8, block), jnp.float32),
        ],
        scratch_shapes=[
            pltpu.VMEM((order_size, width), border.dtype),
            pltpu.VMEM((order_size, width), border.dtype),
        ],
        compiler_params=pltpu.CompilerParams(vmem_limit_bytes=56 * MIB),
    )(touched, live_count, regular_rows, inv_factor[0], border[0])

    def along_place(array, k):
        pairs = [(s, (s // ratio ^ k) * ratio + s % ratio) for s in range(scen_count)]
        return lax.ppermute(array, "scen", pairs)

    def along_tile(array, k):
        return lax.ppermute(array, "tile", [(t, t ^ k) for t in range(tile_count)])

    def along_part(array, k):
        pairs = [(s, s // ratio * ratio + (s % ratio ^ k)) for s in range(scen_count)]
        return lax.ppermute(array, "scen", pairs)

    def gather_plane(array):
        here = [array] + [along_tile(array, k) for k in range(1, tile_count)]
        here = jnp.concatenate(here)
        return [here] + [along_part(here, k) for k in range(1, ratio)]

    corners = [corner] + [along_place(corner, k) for k in range(1, groups)]
    corners = gather_plane(jnp.stack(corners))
    strips = [strip[0]] + [along_place(strip[k], k) for k in range(1, groups)]
    strips = gather_plane(jnp.stack(strips))
    teams = [
        [(z * ratio + c) * tile_count + t for z in range(groups) for t in range(tile_count)]
        for c in range(ratio)
    ]
    blocks = lax.all_to_all(main, both, 0, 0, tiled=True, axis_index_groups=teams)
    blocks = [blocks] + [along_part(blocks, k) for k in range(1, ratio)]

    labels = jnp.concatenate([piece[:, block + batch, :groups] for piece in corners]).astype(jnp.int32)

    tall, wide = row_span * block, group_size * block
    row_id = scen_index * tall + lax.broadcasted_iota(jnp.int32, (tall, wide), 0)
    col_id = tile_index * wide + lax.broadcasted_iota(jnp.int32, (tall, wide), 1)
    background = jnp.where(row_id == col_id, regular[:, None], 0.0)

    inverse = pl.pallas_call(
        functools.partial(factor_kernel, batch, block),
        in_specs=[SMEM] + [VMEM] * len(corners),
        out_specs=VMEM,
        out_shape=jax.ShapeDtypeStruct((batch * block, block), jnp.float32),
        scratch_shapes=[
            pltpu.VMEM((batch * block, block), jnp.float32),
            pltpu.VMEM((batch * PIVOTS, block), jnp.float32),
            pltpu.VMEM((batch * PIVOTS, block), jnp.float32),
        ],
        compiler_params=pltpu.CompilerParams(vmem_limit_bytes=48 * MIB),
    )(labels, *corners)

    panel = pl.pallas_call(
        functools.partial(panel_kernel, batch, block, ratio),
        in_specs=[SMEM, VMEM, VMEM] + [VMEM] * len(strips),
        out_specs=VMEM,
        out_shape=jax.ShapeDtypeStruct((row_share, batch * block), jnp.float32),
        scratch_shapes=[pltpu.VMEM((batch, row_share, block), jnp.float32)],
        compiler_params=pltpu.CompilerParams(vmem_limit_bytes=48 * MIB),
    )(labels, regular_rows, inverse, *strips)

    count = ratio * blocks[0].shape[0]
    schur = pl.pallas_call(
        functools.partial(scatter_kernel, block, ratio),
        in_specs=[SMEM, VMEM] + [VMEM] * len(blocks) + [ANY],
        out_specs=ANY,
        out_shape=jax.ShapeDtypeStruct((tall, wide), jnp.float32),
        input_output_aliases={2 + len(blocks): 0},
        scratch_shapes=[
            pltpu.VMEM((count, block, block), jnp.float32),
            pltpu.SMEM((row_span * group_size,), jnp.int32),
            pltpu.SMEM((count,), jnp.int32),
            pltpu.SemaphoreType.DMA((count,)),
        ],
        compiler_params=pltpu.CompilerParams(vmem_limit_bytes=48 * MIB),
    )(labels, regular_rows, *blocks, background)
    return (schur, panel)


def solution(mesh):
    return jax.shard_map(
        local,
        mesh=mesh,
        in_specs=(
            P(("scen", "tile"), None, None),
            P(("scen", "tile"), None, None),
            P(("scen", "tile"), None),
            P(("scen", "tile")),
            P("scen"),
        ),
        out_specs=(P("scen", "tile"), P(("scen", "tile"), None)),
        check_vma=False,
    )
```

time: 766 us -> 112 us (0.15); the launches traced: 756 us -> 111 us
  other arithmetic: 311 us -> 11.7 us
  local copies, waits for them, and re-layouts: 171 us -> 5.04 us
  waiting for transfers between devices: 177 us -> 32.6 us
  matrix products: 57.5 us -> 0 us
  Pallas kernels: 0 us -> 29 us
  between operations: 20.9 us -> 1.43 us
  starting transfers between devices: 18.7 us -> 31.6 us
    another operation x34 -> x2, other arithmetic: 252 us -> 0.05 us  [the longest x1 0.03 us: local(): corners = gather_plane(jnp.stack(corners))]
    psum x2 -> x0, waiting for transfers between devices: 100 us -> none  [from_root(): return lax.psum(jnp.where(mine, array, jnp.zeros_like(array)), axis)]
    all_to_all x4 -> x1, waiting for transfers between devices: 76.6 us -> 0.01 us  [local(): lax.all_to_all(main, both, 0, 0, tiled=True, axis_index_groups=teams)]
    unnamed x14 -> x17, local copies, waits for them, and re-layouts: 71.8 us -> 3.4 us
    transpose x2 -> x0, local copies, waits for them, and re-layouts: 56.6 us -> none  [local(): summed.reshape(row_span, col_span, block_size, block_size)]
    another operation x29 -> x0, matrix products: 50.5 us -> none  [the longest x14 27.2 us: local(): corner_factor = jnp.linalg.cholesky(corner)]
    another operation x69 -> x0, local copies, waits for them, and re-layouts: 32.9 us -> none
    ppermute x0 -> x15, waiting for transfers between devices: none -> 32.6 us  [the longest x6 18.5 us: along_place(): return lax.ppermute(array, 'scen', pairs)]
  transfers between devices with their start and end apart: 6 -> 16, of which waited for: 4 -> 4; matrix products, arithmetic and copies ran while one was open for 49% -> 15% of each run, Pallas kernels for 0% -> 14%
where the time goes in v1:
time: 112 us; the launch traced here: 111 us
  waiting for transfers between devices  32.6 us (29%)
  starting transfers between devices  31.6 us (28%)
  Pallas kernels  29 us (26%)
  other arithmetic  11.7 us (10%)
  local copies, waits for them, and re-layouts  5.04 us (4%)
  between operations  1.43 us (1%)
    ppermute x6, waiting for transfers between devices, along_place(): return lax.ppermute(array, 'scen', pairs)  18.5 us
    ppermute x6, starting transfers between devices, along_place(): return lax.ppermute(array, 'scen', pairs)  16.7 us
    ppermute x6, waiting for transfers between devices, along_tile(): return lax.ppermute(array, 'tile', [(t, t ^ k) for t in range(tile_count)])  14.1 us
    select_n x1, other arithmetic, local(): background = jnp.where(row_id == col_id, regular[:, None], 0.0)  11.5 us
    pallas_call x1, Pallas kernels, local(): pl.pallas_call(functools.partial(factor_kernel, batch, block), in_specs=[...  10.8 us
    ppermute x6, starting transfers between devices, along_tile(): return lax.ppermute(array, 'tile', [(t, t ^ k) for t in range(tile_count)])  8.02 us
    pallas_call x1, Pallas kernels, local(): pl.pallas_call(functools.partial(scatter_kernel, block, ratio), in_specs=...  7.29 us
    all_to_all x1, starting transfers between devices, local(): lax.all_to_all(main, both, 0, 0, tiled=True, axis_index_groups=teams)  6.32 us
  transfers between devices with their start and end apart: 16, of which 4 were waited for; matrix products, arithmetic and copies ran while one was open for 15% of the time, Pallas kernels for 14%

profile of v1, /device:TPU:0, one launch (start us, length us, event | category | flops | bytes accessed | tf_op | source)
XLA Modules:
  0.0 111.4 jit_solution(4877016094857390635)
XLA Ops:
  1.3 5.9 %shard_map.68 = (f32[16,128,128]{2,1,0:T(8,128)}, f32[4,128,128]{2,1,0:T(8,128)}, f32[144,128]{1,0:T(8,128)}) custom-call(s32[1,4]{1,0:T(1,128)} %touched_ref.1, s32[1]{0:T(128)S(6)} %copy.28.live_ref, f32[16,128]{1,0:T(8,128)} %bitcast.25, bf16[1024,1024]{1,0:T(8,128)(2,1)} %bitcast.28, bf16[1024,512]{1,0:T(8,128)(2,1)} %bitcast.29), custom_call_target="tpu_custom_call" | custom-call | tf_op jit(solution)/shard_map/pallas_call | solution.py:311
  7.2 0.0 copy-start.2
  7.2 5.0 %collective-permute-start.2 = (f32[144,128]{1,0:T(8,128)}, f32[144,128]{1,0:T(8,128)S(1)}, u32[]{:S(2)}, u32[]{:S(2)}) collective-permute-start(f32[144,128]{1,0:T(8,128)} %get-tuple-element.5), channel_id=1, source_target_pairs={{0,24},{4,28},{8,16},{12,20},{16,8},{20,12},{24,0},{28,4},{1,25},{... | collective-permute-start | bytes 221192 | tf_op jit(solution)/shard_map/ppermute | solution.py:339
  12.3 0.0 collective-permute-start.1
  12.3 0.0 copy-start.1
  12.3 6.3 %all-to-all-start = ((f32[16,128,128]{2,1,0:T(8,128)}), f32[16,128,128]{2,1,0:T(8,128)S(1)}, u32[]{:S(2)}, u32[]{:S(2)}) async-start(f32[16,128,128]{2,1,0:T(8,128)} %get-tuple-element.6), calls=%async_computation | async-start | bytes 2097152 | tf_op jit(solution)/shard_map/all_to_all | solution.py:361
  18.6 0.0 copy-done.2
  18.6 0.6 fusion
  19.3 3.7 %collective-permute-start.10 = (f32[128,128]{1,0:T(8,128)S(1)}, f32[128,128]{1,0:T(8,128)S(1)}, u32[]{:S(2)}, u32[]{:S(2)}) collective-permute-start(f32[128,128]{1,0:T(8,128)S(1)} %get-tuple-element.10), channel_id=1, source_target_pairs={{0,24},{4,28},{8,16},{12,20},{16,8},{20,12},{24,0},{28,4},{1,25},{... | collective-permute-start | bytes 196616 | tf_op jit(solution)/shard_map/ppermute | solution.py:339
  23.0 0.0 collective-permute-start.9
  23.0 0.7 collective-permute-start.8
  23.7 0.0 copy-done.1
  23.7 18.3 %collective-permute-done.10 = f32[128,128]{1,0:T(8,128)S(1)} collective-permute-done((f32[128,128]{1,0:T(8,128)S(1)}, f32[128,128]{1,0:T(8,128)S(1)}, u32[]{:S(2)}, u32[]{:S(2)}) %collective-permute-start.10) | collective-permute-done | bytes 65568 | tf_op jit(solution)/shard_map/ppermute | solution.py:339
  42.0 7.3 %collective-permute-start = (f32[144,128]{1,0:T(8,128)S(1)}, f32[144,128]{1,0:T(8,128)S(1)}, u32[]{:S(2)}, u32[]{:S(2)}) collective-permute-start(f32[144,128]{1,0:T(8,128)S(1)} %copy-done.1), channel_id=1, source_target_pairs={{0,8},{4,12},{8,0},{12,4},{16,24},{20,28},{24,16},{28,20},{1,9},{5... | collective-permute-start | bytes 221192 | tf_op jit(solution)/shard_map/ppermute | solution.py:339
  49.2 0.2 collective-permute-done.9
  49.5 0.0 collective-permute-done.8
  49.5 2.5 %collective-permute-start.13 = (f32[4,128,128]{2,1,0:T(8,128)S(1)}, f32[4,128,128]{2,1,0:T(8,128)S(1)}, u32[]{:S(2)}, u32[]{:S(2)}) collective-permute-start(f32[4,128,128]{2,1,0:T(8,128)S(1)} %pad_maximum_fusion.1), channel_id=1, source_target_pairs={{0,3},{1,2},{2,1},{3,0},{4,7},{5,6},{6,5},{7,4},{8,11},{9,10},{10,... | collective-permute-start | bytes 786440 | tf_op jit(solution)/shard_map/ppermute | solution.py:342
  52.0 0.5 collective-permute-start.12
  52.5 0.6 constant_dynamic-update-slice_fusion.12
  53.1 0.6 constant_dynamic-update-slice_fusion.11
  53.8 0.6 constant_dynamic-update-slice_fusion.10
  54.4 0.0 collective-permute-done.2
  54.4 0.6 collective-permute-start.11
  55.0 0.0 collective-permute-done.1
  55.0 0.0 collective-permute-done
  55.0 2.5 %collective-permute-start.5 = (f32[4,144,128]{2,1,0:T(8,128)S(1)}, f32[4,144,128]{2,1,0:T(8,128)S(1)}, u32[]{:S(2)}, u32[]{:S(2)}) collective-permute-start(f32[4,144,128]{2,1,0:T(8,128)S(1)} %pad_maximum_fusion), channel_id=1, source_target_pairs={{0,3},{1,2},{2,1},{3,0},{4,7},{5,6},{6,5},{7,4},{8,11},{9,10},{10,... | collective-permute-start | bytes 884744 | tf_op jit(solution)/shard_map/ppermute | solution.py:342
  57.5 0.5 collective-permute-start.4
  58.0 7.4 %collective-permute-done.11 = f32[4,128,128]{2,1,0:T(8,128)S(1)} collective-permute-done((f32[4,128,128]{2,1,0:T(8,128)S(1)}, f32[4,128,128]{2,1,0:T(8,128)S(1)}, u32[]{:S(2)}, u32[]{:S(2)}) %collective-permute-start.11) | collective-permute-done | bytes 262176 | tf_op jit(solution)/shard_map/ppermute | solution.py:342
  65.4 1.5 %collective-permute-start.3 = (f32[4,144,128]{2,1,0:T(8,128)S(1)}, f32[4,144,128]{2,1,0:T(8,128)S(1)}, u32[]{:S(2)}, u32[]{:S(2)}) collective-permute-start(f32[4,144,128]{2,1,0:T(8,128)S(1)} %pad_maximum_fusion), channel_id=1, source_target_pairs={{0,1},{1,0},{2,3},{3,2},{4,5},{5,4},{6,7},{7,6},{8,9},{9,8},{10,11... | collective-permute-start | bytes 884744 | tf_op jit(solution)/shard_map/ppermute | solution.py:342
  66.9 0.7 constant_dynamic-update-slice_fusion.9
  67.6 0.0 collective-permute-done.12
  67.6 0.7 constant_dynamic-update-slice_fusion.8
  68.3 0.0 copy-start
  68.3 0.0 collective-permute-done.13
  68.3 0.7 constant_dynamic-update-slice_fusion.7.refs_0_
  69.0 0.0 collective-permute-start.14
  69.0 6.7 %collective-permute-done.3 = f32[4,144,128]{2,1,0:T(8,128)S(1)} collective-permute-done((f32[4,144,128]{2,1,0:T(8,128)S(1)}, f32[4,144,128]{2,1,0:T(8,128)S(1)}, u32[]{:S(2)}, u32[]{:S(2)}) %collective-permute-start.3) | collective-permute-done | bytes 294944 | tf_op jit(solution)/shard_map/ppermute | solution.py:342
  75.8 0.0 collective-permute-done.4
  75.8 0.0 collective-permute-done.5
  75.8 0.1 collective-permute-start.6
  75.9 0.0 all-to-all-done.refs_0_
  75.9 0.5 collective-permute-start.7
  76.4 0.0 copy-done
  76.4 11.5 %compare_select_fusion.refs_2_ = f32[2048,4096]{1,0:T(8,128)} fusion(f32[2048]{0:T(1024)S(1)} %copy-done, s32[4096]{0:T(1024)S(1)} %iota_add_fusion, s32[2048]{0:T(1024)S(1)} %iota_add_fusion.1), kind=kLoop, calls=%fused_computation | loop fusion | flops 16777216 | bytes 33587200 | tf_op jit(solution)/shard_map/jit(_where)/select_n | solution.py:369
  88.0 0.1 copy.12
  88.0 0.0 collective-permute-done.6.refs_1_
  88.1 0.1 copy.13
  88.1 0.1 pad_maximum_fusion.2
  88.2 0.1 copy.14
  88.3 10.8 %shard_map.70.inverse_ref = f32[1024,128]{1,0:T(8,128)S(1)} custom-call(s32[32,4]{1,0:T(8,128)S(1)} %convert_element_type.3.label_ref, f32[16,144,128]{2,1,0:T(8,128)S(1)} %constant_dynamic-update-slice_fusion.refs_0_, f32[16,144,128]{2,1,0:T(8,128)S(1)} %collective-permute-done.6.refs_1_), custom_call_target="tpu_custom_call" | custom-call | tf_op jit(solution)/shard_map/pallas_call | solution.py:371
  99.2 0.0 collective-permute-done.14.refs_1_
  99.2 4.9 %shard_map.71 = f32[512,1024]{1,0:T(8,128)} custom-call(s32[32,4]{1,0:T(8,128)S(1)} %convert_element_type.3.label_ref, f32[16,128]{1,0:T(8,128)S(1)} %bitcast.26, f32[1024,128]{1,0:T(8,128)S(1)} %shard_map.70.inverse_ref, f32[16,128,128]{2,1,0:T(8,128)} %constant_dynamic-update-slice_fusion.7.refs_0_, f32[16,128,128]{2,1,0:T(8,128)} %collective-permute-done.14.refs_1_), custom_call_target="tpu_custom_call" | custom-call | tf_op jit(solution)/shard_map/pallas_call | solution.py:384
  104.1 0.0 collective-permute-done.7.refs_1_
  104.1 7.3 %shard_map.69 = f32[2048,4096]{1,0:T(8,128)} custom-call(s32[32,4]{1,0:T(8,128)S(1)} %convert_element_type.3.label_ref, f32[16,128]{1,0:T(8,128)S(1)} %bitcast.27, f32[16,128,128]{2,1,0:T(8,128)S(1)} %all-to-all-done.refs_0_, f32[16,128,128]{2,1,0:T(8,128)} %collective-permute-done.7.refs_1_, ...), custom_call_target="tpu_custom_call", output_to_operand_aliasing={{}: (4, {})} | custom-call | tf_op jit(solution)/shard_map/pallas_call | solution.py:394
  (14 shorter events, 0.2 us)
Async XLA Ops:
  7.2 11.4 %copy-start.2 = (f32[4,128,128]{2,1,0:T(8,128)S(1)}, f32[4,128,128]{2,1,0:T(8,128)}, u32[]{:S(2)}) copy-start(f32[4,128,128]{2,1,0:T(8,128)} %get-tuple-element.7) | copy-start | bytes 786436
  7.2 47.2 %collective-permute-start.2 = (f32[144,128]{1,0:T(8,128)}, f32[144,128]{1,0:T(8,128)S(1)}, u32[]{:S(2)}, u32[]{:S(2)}) collective-permute-start(f32[144,128]{1,0:T(8,128)} %get-tuple-element.5), channel_id=1, source_target_pairs={{0,24},{4,28},{8,16},{12,20},{16,8},{20,12},{24,0},{28,4},{1,25},{... | collective-permute-start | bytes 221192 | tf_op jit(solution)/shard_map/ppermute | solution.py:339
  12.3 42.7 %collective-permute-start.1 = (f32[144,128]{1,0:T(8,128)}, f32[144,128]{1,0:T(8,128)S(1)}, u32[]{:S(2)}, u32[]{:S(2)}) collective-permute-start(f32[144,128]{1,0:T(8,128)} %get-tuple-element.5), channel_id=1, source_target_pairs={{0,16},{4,20},{8,24},{12,28},{16,0},{20,4},{24,8},{28,12},{1,17},{... | collective-permute-start | bytes 221192 | tf_op jit(solution)/shard_map/ppermute | solution.py:339
  12.3 11.4 %copy-start.1 = (f32[144,128]{1,0:T(8,128)S(1)}, f32[144,128]{1,0:T(8,128)}, u32[]{:S(2)}) copy-start(f32[144,128]{1,0:T(8,128)} %get-tuple-element.5) | copy-start | bytes 221188
  12.3 63.6 %all-to-all-start = ((f32[16,128,128]{2,1,0:T(8,128)}), f32[16,128,128]{2,1,0:T(8,128)S(1)}, u32[]{:S(2)}, u32[]{:S(2)}) async-start(f32[16,128,128]{2,1,0:T(8,128)} %get-tuple-element.6), calls=%async_computation | async-start | bytes 2097152 | tf_op jit(solution)/shard_map/all_to_all | solution.py:361
  19.3 22.7 %collective-permute-start.10 = (f32[128,128]{1,0:T(8,128)S(1)}, f32[128,128]{1,0:T(8,128)S(1)}, u32[]{:S(2)}, u32[]{:S(2)}) collective-permute-start(f32[128,128]{1,0:T(8,128)S(1)} %get-tuple-element.10), channel_id=1, source_target_pairs={{0,24},{4,28},{8,16},{12,20},{16,8},{20,12},{24,0},{28,4},{1,25},{... | collective-permute-start | bytes 196616 | tf_op jit(solution)/shard_map/ppermute | solution.py:339
  23.0 26.5 %collective-permute-start.9 = (f32[128,128]{1,0:T(8,128)S(1)}, f32[128,128]{1,0:T(8,128)S(1)}, u32[]{:S(2)}, u32[]{:S(2)}) collective-permute-start(f32[128,128]{1,0:T(8,128)S(1)} %get-tuple-element.11), channel_id=1, source_target_pairs={{0,16},{4,20},{8,24},{12,28},{16,0},{20,4},{24,8},{28,12},{1,17},{... | collective-permute-start | bytes 196616 | tf_op jit(solution)/shard_map/ppermute | solution.py:339
  23.0 26.5 %collective-permute-start.8 = (f32[128,128]{1,0:T(8,128)S(1)}, f32[128,128]{1,0:T(8,128)S(1)}, u32[]{:S(2)}, u32[]{:S(2)}) collective-permute-start(f32[128,128]{1,0:T(8,128)S(1)} %get-tuple-element.12), channel_id=1, source_target_pairs={{0,8},{4,12},{8,0},{12,4},{16,24},{20,28},{24,16},{28,20},{1,9},{5... | collective-permute-start | bytes 196616 | tf_op jit(solution)/shard_map/ppermute | solution.py:339
  42.0 13.0 %collective-permute-start = (f32[144,128]{1,0:T(8,128)S(1)}, f32[144,128]{1,0:T(8,128)S(1)}, u32[]{:S(2)}, u32[]{:S(2)}) collective-permute-start(f32[144,128]{1,0:T(8,128)S(1)} %copy-done.1), channel_id=1, source_target_pairs={{0,8},{4,12},{8,0},{12,4},{16,24},{20,28},{24,16},{28,20},{1,9},{5... | collective-permute-start | bytes 221192 | tf_op jit(solution)/shard_map/ppermute | solution.py:339
  49.5 18.8 %collective-permute-start.13 = (f32[4,128,128]{2,1,0:T(8,128)S(1)}, f32[4,128,128]{2,1,0:T(8,128)S(1)}, u32[]{:S(2)}, u32[]{:S(2)}) collective-permute-start(f32[4,128,128]{2,1,0:T(8,128)S(1)} %pad_maximum_fusion.1), channel_id=1, source_target_pairs={{0,3},{1,2},{2,1},{3,0},{4,7},{5,6},{6,5},{7,4},{8,11},{9,10},{10,... | collective-permute-start | bytes 786440 | tf_op jit(solution)/shard_map/ppermute | solution.py:342
  52.0 15.6 %collective-permute-start.12 = (f32[4,128,128]{2,1,0:T(8,128)S(1)}, f32[4,128,128]{2,1,0:T(8,128)S(1)}, u32[]{:S(2)}, u32[]{:S(2)}) collective-permute-start(f32[4,128,128]{2,1,0:T(8,128)S(1)} %pad_maximum_fusion.1), channel_id=1, source_target_pairs={{0,2},{1,3},{2,0},{3,1},{4,6},{5,7},{6,4},{7,5},{8,10},{9,11},{10,... | collective-permute-start | bytes 786440 | tf_op jit(solution)/shard_map/ppermute | solution.py:342
  54.4 11.0 %collective-permute-start.11 = (f32[4,128,128]{2,1,0:T(8,128)S(1)}, f32[4,128,128]{2,1,0:T(8,128)S(1)}, u32[]{:S(2)}, u32[]{:S(2)}) collective-permute-start(f32[4,128,128]{2,1,0:T(8,128)S(1)} %pad_maximum_fusion.1), channel_id=1, source_target_pairs={{0,1},{1,0},{2,3},{3,2},{4,5},{5,4},{6,7},{7,6},{8,9},{9,8},{10,11... | collective-permute-start | bytes 786440 | tf_op jit(solution)/shard_map/ppermute | solution.py:342
  55.0 20.8 %collective-permute-start.5 = (f32[4,144,128]{2,1,0:T(8,128)S(1)}, f32[4,144,128]{2,1,0:T(8,128)S(1)}, u32[]{:S(2)}, u32[]{:S(2)}) collective-permute-start(f32[4,144,128]{2,1,0:T(8,128)S(1)} %pad_maximum_fusion), channel_id=1, source_target_pairs={{0,3},{1,2},{2,1},{3,0},{4,7},{5,6},{6,5},{7,4},{8,11},{9,10},{10,... | collective-permute-start | bytes 884744 | tf_op jit(solution)/shard_map/ppermute | solution.py:342
  57.5 18.3 %collective-permute-start.4 = (f32[4,144,128]{2,1,0:T(8,128)S(1)}, f32[4,144,128]{2,1,0:T(8,128)S(1)}, u32[]{:S(2)}, u32[]{:S(2)}) collective-permute-start(f32[4,144,128]{2,1,0:T(8,128)S(1)} %pad_maximum_fusion), channel_id=1, source_target_pairs={{0,2},{1,3},{2,0},{3,1},{4,6},{5,7},{6,4},{7,5},{8,10},{9,11},{10,... | collective-permute-start | bytes 884744 | tf_op jit(solution)/shard_map/ppermute | solution.py:342
  65.4 10.3 %collective-permute-start.3 = (f32[4,144,128]{2,1,0:T(8,128)S(1)}, f32[4,144,128]{2,1,0:T(8,128)S(1)}, u32[]{:S(2)}, u32[]{:S(2)}) collective-permute-start(f32[4,144,128]{2,1,0:T(8,128)S(1)} %pad_maximum_fusion), channel_id=1, source_target_pairs={{0,1},{1,0},{2,3},{3,2},{4,5},{5,4},{6,7},{7,6},{8,9},{9,8},{10,11... | collective-permute-start | bytes 884744 | tf_op jit(solution)/shard_map/ppermute | solution.py:342
  68.3 8.1 %copy-start = (f32[2048]{0:T(1024)S(1)}, f32[2048]{0:T(1024)}, u32[]{:S(2)}) copy-start(f32[2048]{0:T(1024)} %param.9) | copy-start | bytes 24580
  69.0 30.1 %collective-permute-start.14 = (f32[16,128,128]{2,1,0:T(8,128)}, f32[16,128,128]{2,1,0:T(8,128)}, u32[]{:S(2)}, u32[]{:S(2)}) collective-permute-start(f32[16,128,128]{2,1,0:T(8,128)} %constant_dynamic-update-slice_fusion.7.refs_0_), channel_id=1, source_target_pairs={{0,4},{4,0},{8,12},{12,8},{16,20},{20,16},{24,28},{28,24},{1,5},{5... | collective-permute-start | bytes 3145736 | tf_op jit(solution)/shard_map/ppermute | solution.py:346
  75.8 12.2 %collective-permute-start.6 = (f32[16,144,128]{2,1,0:T(8,128)S(1)}, f32[16,144,128]{2,1,0:T(8,128)S(1)}, u32[]{:S(2)}, u32[]{:S(2)}) collective-permute-start(f32[16,144,128]{2,1,0:T(8,128)S(1)} %constant_dynamic-update-slice_fusion.refs_0_), channel_id=1, source_target_pairs={{0,4},{4,0},{8,12},{12,8},{16,20},{20,16},{24,28},{28,24},{1,5},{5... | collective-permute-start | bytes 3538952 | tf_op jit(solution)/shard_map/ppermute | solution.py:346
  75.9 28.2 %collective-permute-start.7 = (f32[16,128,128]{2,1,0:T(8,128)S(1)}, f32[16,128,128]{2,1,0:T(8,128)}, u32[]{:S(2)}, u32[]{:S(2)}) collective-permute-start(f32[16,128,128]{2,1,0:T(8,128)S(1)} %all-to-all-done.refs_0_), channel_id=1, source_target_pairs={{0,4},{4,0},{8,12},{12,8},{16,20},{20,16},{24,28},{28,24},{1,5},{5... | collective-permute-start | bytes 3145736 | tf_op jit(solution)/shard_map/ppermute | solution.py:346

commit v2 on v1

v2 whole, which is shorter than its diff:
```python
import functools
import math

import jax
import jax.numpy as jnp
from jax import lax
from jax.experimental import pallas as pl
from jax.experimental.pallas import tpu as pltpu
from jax.sharding import PartitionSpec as P

FIRST = 16384
PANEL = 1024
PIVOTS = 8
ZEROS = 64
MIB = 1 << 20

SMEM = pl.BlockSpec(memory_space=pltpu.SMEM)
VMEM = pl.BlockSpec(memory_space=pltpu.VMEM)
ANY = pl.BlockSpec(memory_space=pl.ANY)
HBM = pl.BlockSpec(memory_space=pltpu.HBM)


def gram(left, right):
    return lax.dot_general(left, right, (((0,), (0,)), ((), ())), preferred_element_type=jnp.float32)


def fill(zero_scr, back_ref, sems):
    tall = zero_scr.shape[0]
    zero_scr[...] = jnp.zeros_like(zero_scr)
    copies = [
        pltpu.make_async_copy(zero_scr, back_ref.at[i * tall:(i + 1) * tall], sems.at[i])
        for i in range(back_ref.shape[0] // tall)
    ]
    for copy in copies:
        copy.start()
    return copies


def first_kernel(
    groups, block, group_size, ratio, touched_ref, live_ref, regular_ref, inv_ref, border_ref,
    scaled_ref, *refs,
):
    *first_refs, inv_scr, border_scr, column_scr, inv_sem, border_sems = refs
    place = lax.axis_index("scen") // ratio
    copies = []
    keeps, labels = [], []
    for group in range(groups):
        slot = jnp.int32(0)
        for m in range(groups):
            slot = jnp.where(touched_ref[0, m] // group_size == group, m, slot)
        copies.append(pltpu.make_async_copy(
            border_ref.at[:, pl.ds(pl.multiple_of(slot * block, block), block)],
            border_scr.at[:, group * block:(group + 1) * block],
            border_sems.at[group],
        ))
        keeps.append(slot < live_ref[0])
        labels.append(jnp.where(slot < live_ref[0], touched_ref[0, slot], -1).astype(jnp.float32))
    copies.append(pltpu.make_async_copy(inv_ref, inv_scr, inv_sem))
    for copy in copies:
        copy.start()
    keep = jnp.concatenate(
        [jnp.broadcast_to(keep.astype(jnp.float32), (1, block)) for keep in keeps], axis=1
    )
    for copy in copies:
        copy.wait()
    scaled = jnp.dot(inv_scr[...], border_scr[...], preferred_element_type=jnp.float32)
    scaled_ref[...] = jnp.where(keep > 0.0, scaled, 0.0).astype(scaled_ref.dtype)
    strip = gram(scaled_ref[:, :block], scaled_ref[...])
    half = block // 2
    corner_rows = first_refs[0].shape[0] - block
    corner = pack_corner(groups, strip[:, :block])
    is_root = (lax.axis_index("scen") == 0) & (lax.axis_index("tile") == 0)
    root_rows = regular_ref[:corner_rows - half - 8, :] * is_root.astype(jnp.float32)
    lane = lax.broadcasted_iota(jnp.int32, (8, block), 1)
    last = corner[half:]
    for group in range(groups):
        column_scr[group] = strip[:, group * block:(group + 1) * block].T
        last = jnp.where(lane == group, labels[group], last)
    for k in range(groups):
        first_refs[k][:half] = corner[:half]
        first_refs[k][half:half + 8] = last
        first_refs[k][half + 8:corner_rows] = root_rows
        first_refs[k][corner_rows:] = column_scr[place ^ k]


def main_kernel(groups, block, scaled_ref, main_ref):
    for group in range(groups):
        strip = gram(scaled_ref[:, group * block:(group + 1) * block], scaled_ref[...])
        for other in range(groups):
            main_ref[group * groups + other] = strip[:, other * block:(other + 1) * block]


def pack_corner(groups, whole):
    block = whole.shape[0]
    half = block // 2
    assert groups <= half
    row_id = lax.broadcasted_iota(jnp.int32, (half, block), 0)
    col_id = lax.broadcasted_iota(jnp.int32, (half, block), 1)
    upper, lower = whole[:half], whole[half:]
    body = jnp.where(col_id >= row_id, upper, pltpu.roll(lower, half, 1))
    ends = jnp.sum(jnp.where(col_id == row_id + half, lower, 0.0), axis=0, keepdims=True)
    return jnp.concatenate([body, jnp.broadcast_to(ends, (8, block))])


def unpack_upper(block, packed, ends):
    half = block // 2
    row_id = lax.broadcasted_iota(jnp.int32, (half, block), 0)
    col_id = lax.broadcasted_iota(jnp.int32, (half, block), 1)
    low = jnp.where(col_id < row_id, packed, 0.0)
    turned = jnp.concatenate([low, jnp.zeros_like(low)]).T[:half]
    lower = pltpu.roll(turned, half, 1) + jnp.where(col_id == row_id + half, ends, 0.0)
    return jnp.concatenate([packed, lower])


def pivot_rows(rows, start, lane):
    count = len(rows)
    entry = {}
    for b in range(count):
        at = jnp.full(lane.shape, start + b, jnp.int32)
        for a in range(b + 1):
            entry[a, b] = jnp.take_along_axis(rows[a], at, axis=1, mode="promise_in_bounds")
    lower = {}
    for a in range(count):
        lower[a, a] = 1.0 / entry[a, a]
        for b in range(a + 1, count):
            lower[b, a] = entry[a, b] * lower[a, a]
            for c in range(b, count):
                entry[b, c] = entry[b, c] - lower[b, a] * entry[a, c]
    whole, mults, pivots, done = [], [], [], []
    for a in range(count):
        row = rows[a]
        for b in range(a):
            row = jnp.where(lane == start + b, 0.0, row) - lower[a, b] * whole[b]
        mults.append(jnp.where(lane >= start + count, row * lower[a, a], 0.0))
        whole.append(jnp.where(lane == start + a, 1.0, row))
        pivots.append(jnp.where((lane > start + a) & (lane < start + count), 0.0, whole[a]))
        done.append(jnp.where(lane <= start + a, whole[a] * lax.rsqrt(entry[a, a]), 0.0))
    return mults, pivots, done


def split_three(value):
    high = value.astype(jnp.bfloat16).astype(jnp.float32)
    rest = value - high
    middle = rest.astype(jnp.bfloat16).astype(jnp.float32)
    return high, middle, rest - middle


def factor_kernel(batch, block, ratio, share, *refs):
    (*piece_refs, out_ref, back_ref, plan_ref, spot_ref,
     packed_scr, sum_scr, mult_scr, pivot_scr, zero_scr, label_scr, owner_scr, sems) = refs
    half = block // 2
    scen, tile = lax.axis_index("scen"), lax.axis_index("tile")
    tile_count = lax.axis_size("tile")
    place = scen // ratio
    tall, wide = back_ref.shape[0] // block, back_ref.shape[1] // block
    count, groups = label_scr.shape
    turns = block // PIVOTS
    per_turn = -(-count // turns)
    assert count % turns == 0
    nowhere = tall * wide
    device_row = (scen * tile_count + tile) * share

    def claim(i):
        part, sent = i // (tile_count * groups), i % (tile_count * groups)
        sender = part * (tile_count * groups) + ((sent % tile_count) ^ tile) * groups + ((sent // tile_count) ^ place)
        row, column = label_scr[sender, place], label_scr[sender, tile]
        inside = (row >= scen * tall) & (row < (scen + 1) * tall) & (column >= 0)
        spot = jnp.where(inside, (row - scen * tall) * wide + column - tile * wide, nowhere)
        owner = owner_scr[spot]
        owner = jnp.where(inside, jnp.where(owner < 0, i, owner), -1)
        owner_scr[spot] = owner
        plan_ref[0, i] = owner
        spot_ref[i] = jnp.where(owner == i, spot, -1)
        row, column = label_scr[i, place] * block, label_scr[i, 0]
        wanted = (column >= 0) & (column < batch) & (row >= 0)
        wanted = wanted & (row < device_row + share) & (device_row < row + block)
        plan_ref[1, i] = jnp.where(wanted, jnp.maximum(row - device_row, 0) // block * batch + column, -1)

    copies = fill(zero_scr, back_ref, sems)
    for i in range(nowhere + 1):
        owner_scr[i] = -1
    for i in range(tall):
        column = scen * tall + i - tile * wide
        spot = jnp.where((column >= 0) & (column < wide), i * wide + column, nowhere)
        owner_scr[spot] = count + i
        spot_ref[count + i] = jnp.where(spot < nowhere, spot, -1)
    packed_scr[...] = jnp.zeros_like(packed_scr)
    diagonal = jnp.zeros((batch, block), jnp.float32)
    base = 0
    for piece in piece_refs:
        for i in range(piece.shape[0]):
            diagonal = diagonal + piece[i, half + 8:half + 8 + batch, :]
            for group in range(groups):
                label_scr[base + i, group] = piece[i, half, group].astype(jnp.int32)
        base += piece.shape[0]
    base = 0
    for piece in piece_refs:

        def add_one(i, unused, piece=piece, base=base):
            label = label_scr[base + i, 0]

            @pl.when((label >= 0) & (label < batch))
            def add():
                packed_scr[label] += piece[i, :half + 8, :]

            return unused

        lax.fori_loop(0, piece.shape[0], add_one, 0)
        base += piece.shape[0]
    row_id = lax.broadcasted_iota(jnp.int32, (block, block), 0)
    col_id = lax.broadcasted_iota(jnp.int32, (block, block), 1)
    for j in range(batch):
        values = unpack_upper(block, packed_scr[j, :half], packed_scr[j, half:half + 1])
        sum_scr[j * block:(j + 1) * block, :] = values + jnp.where(row_id == col_id, diagonal[j:j + 1, :], 0.0)
    lane = lax.broadcasted_iota(jnp.int32, (batch, block), 1)

    def eliminate(turn, unused):
        start = turn * PIVOTS
        rows = [sum_scr[pl.ds(start + a, batch, stride=block), :] for a in range(PIVOTS)]
        mults, pivots, done = pivot_rows(rows, start, lane)
        for a in range(PIVOTS):
            at = slice(a * batch, (a + 1) * batch)
            out_ref[pl.ds(start + a, batch, stride=block), :] = done[a]
            mult_scr[at, :] = mults[a]
            pivot_scr[at, :] = pivots[a]
        for n in range(per_turn):
            claim(turn * per_turn + n)
        pivot_lane = (col_id >= start) & (col_id < start + PIVOTS)
        for j in range(batch):
            high, middle, low = split_three(mult_scr[pl.ds(j, PIVOTS, stride=batch), :])
            left = jnp.concatenate([high, high, middle, high, middle, low])
            high, middle, low = split_three(pivot_scr[pl.ds(j, PIVOTS, stride=batch), :])
            right = jnp.concatenate([high, middle, high, low, middle, high])
            change = lax.dot_general(
                left.astype(jnp.bfloat16), right.astype(jnp.bfloat16),
                (((0,), (0,)), ((), ())), preferred_element_type=jnp.float32,
            )
            at = slice(j * block, (j + 1) * block)
            sum_scr[at, :] = jnp.where(pivot_lane, 0.0, sum_scr[at, :]) - change
        return unused

    lax.fori_loop(0, turns, eliminate, 0)
    for copy in copies:
        copy.wait()


def split(value):
    high = value.astype(jnp.bfloat16)
    low = (value - high.astype(jnp.float32)).astype(jnp.bfloat16)
    return high, low


def panel_kernel(batch, block, plan_ref, regular_ref, inverse_ref, *refs):
    *piece_refs, out_ref, sum_scr, out_scr, sems = refs
    share = out_ref.shape[0]
    tall = min(share, block)
    first_row = (lax.axis_index("scen") * lax.axis_size("tile") + lax.axis_index("tile")) * share
    sum_scr[...] = jnp.zeros_like(sum_scr)
    base = 0
    for piece in piece_refs:
        for i in range(piece.shape[0]):
            spot = plan_ref[1, base + i]

            @pl.when(spot >= 0)
            def add(piece=piece, i=i, spot=spot):
                at = pl.multiple_of(spot // batch * tall, tall)
                piece_at = pl.multiple_of(first_row % block // tall * tall, tall)
                sum_scr[spot % batch, pl.ds(at, tall), :] += piece[i, pl.ds(piece_at, tall), :]

        base += piece.shape[0]

    @pl.when(first_row < batch * block)
    def add_diagonal():
        for j in range(batch):
            row_id = first_row + lax.broadcasted_iota(jnp.int32, (share, block), 0)
            col_id = j * block + lax.broadcasted_iota(jnp.int32, (share, block), 1)
            sum_scr[j] += jnp.where(row_id == col_id, regular_ref[j:j + 1, :], 0.0)

    copies = []
    for j in range(batch):
        at = slice(j * block, (j + 1) * block)
        left = jnp.concatenate(split(sum_scr[j]), axis=1)
        high, low = split(inverse_ref[at, :])
        right = jnp.concatenate([
            jnp.concatenate([high, high], axis=1),
            jnp.concatenate([low, jnp.zeros_like(low)], axis=1),
        ])
        product = lax.dot_general(
            left, right, (((1,), (1,)), ((), ())), preferred_element_type=jnp.float32
        )
        out_scr[j] = product[:, :block] + product[:, block:]
        copies.append(pltpu.make_async_copy(out_scr.at[j], out_ref.at[:, at], sems.at[j]))
        copies[-1].start()
    for copy in copies:
        copy.wait()


def scatter_kernel(block, plan_ref, spot_ref, regular_ref, *refs):
    *piece_refs, back_ref, out_ref, sum_scr, sems = refs
    row_id = lax.broadcasted_iota(jnp.int32, (block, block), 0)
    col_id = lax.broadcasted_iota(jnp.int32, (block, block), 1)
    tall, wide = out_ref.shape[0] // block, out_ref.shape[1] // block
    count = sum(piece.shape[0] for piece in piece_refs)

    def diagonal_one(i, unused):
        @pl.when(spot_ref[count + i] >= 0)
        def put():
            sum_scr[count + i] = jnp.where(row_id == col_id, regular_ref[pl.ds(i, 1), :], 0.0)

        return unused

    lax.fori_loop(0, tall, diagonal_one, 0)
    base = 0
    for piece in piece_refs:

        def add_one(i, unused, piece=piece, base=base):
            owner = plan_ref[0, base + i]

            @pl.when(owner == base + i)
            def put():
                sum_scr[owner] = piece[i]

            @pl.when((owner >= 0) & (owner != base + i))
            def add():
                sum_scr[owner] += piece[i]

            return unused

        lax.fori_loop(0, piece.shape[0], add_one, 0)
        base += piece.shape[0]

    def copy(i):
        spot = spot_ref[i]
        row = pl.multiple_of(spot // wide * block, block)
        column = pl.multiple_of(spot % wide * block, block)
        return pltpu.make_async_copy(
            sum_scr.at[i], out_ref.at[pl.ds(row, block), pl.ds(column, block)], sems.at[i]
        )

    def start_one(i, unused):
        @pl.when(spot_ref[i] >= 0)
        def start():
            copy(i).start()

        return unused

    def wait_one(i, unused):
        @pl.when(spot_ref[i] >= 0)
        def wait():
            copy(i).wait()

        return unused

    lax.fori_loop(0, count + tall, start_one, 0)
    lax.fori_loop(0, count + tall, wait_one, 0)


def limit(*held):
    size = sum(math.prod(one.shape) * jnp.dtype(one.dtype).itemsize for one in held)
    return pltpu.CompilerParams(vmem_limit_bytes=min(size + 4 * MIB, 60 * MIB))


def local(inv_factor, border, touched, live_count, regular):
    scen_count = lax.axis_size("scen")
    tile_count = lax.axis_size("tile")
    scen_index = lax.axis_index("scen")
    tile_index = lax.axis_index("tile")
    local_count, order_size, width = border.shape
    groups = touched.shape[1]
    block = width // groups
    block_total = FIRST // block
    group_size = block_total // groups
    batch = PANEL // block
    ratio = scen_count // groups
    row_span = block_total // scen_count
    row_share = FIRST // (scen_count * tile_count)
    assert local_count == 1 and tile_count == groups and scen_count == groups * ratio
    assert batch <= group_size and batch * block <= regular.shape[0]
    corner_rows = block // 2 + 8 + batch
    both = ("scen", "tile")
    regular_rows = regular.reshape(-1, block)

    tall, wide = row_span * block, group_size * block
    zeros = [pltpu.VMEM((ZEROS, wide), jnp.float32), pltpu.SemaphoreType.DMA((tall // ZEROS,))]

    scaled, *first = pl.pallas_call(
        functools.partial(first_kernel, groups, block, group_size, ratio),
        in_specs=[SMEM, SMEM, VMEM, HBM, HBM],
        out_specs=[VMEM] * (groups + 1),
        out_shape=[jax.ShapeDtypeStruct((order_size, width), border.dtype)]
        + [jax.ShapeDtypeStruct((corner_rows + block, block), jnp.float32)] * groups,
        scratch_shapes=[
            pltpu.VMEM((order_size, order_size), inv_factor.dtype),
            pltpu.VMEM((order_size, width), border.dtype),
            pltpu.VMEM((groups, block, block), jnp.float32),
            pltpu.SemaphoreType.DMA,
            pltpu.SemaphoreType.DMA((groups,)),
        ],
        compiler_params=pltpu.CompilerParams(vmem_limit_bytes=60 * MIB),
    )(touched, live_count, regular_rows, inv_factor[0], border[0])
    main = pl.pallas_call(
        functools.partial(main_kernel, groups, block),
        in_specs=[VMEM],
        out_specs=VMEM,
        out_shape=jax.ShapeDtypeStruct((groups * groups, block, block), jnp.float32),
        compiler_params=limit(scaled, jax.ShapeDtypeStruct((groups * groups, block, block), jnp.float32)),
    )(scaled)
    def along_place(array, k):
        pairs = [(s, (s // ratio ^ k) * ratio + s % ratio) for s in range(scen_count)]
        return lax.ppermute(array, "scen", pairs)

    def along_tile(array, k):
        return lax.ppermute(array, "tile", [(t, t ^ k) for t in range(tile_count)])

    def along_part(array, k):
        pairs = [(s, s // ratio * ratio + (s % ratio ^ k)) for s in range(scen_count)]
        return lax.ppermute(array, "scen", pairs)

    def along_tiles(array):
        return [array] + [along_tile(array, k) for k in range(1, tile_count)]

    def along_parts(pieces):
        return pieces + [along_part(piece, k) for k in range(1, ratio) for piece in pieces]

    firsts = [first[0]] + [along_place(first[k], k) for k in range(1, groups)]
    corners = along_tiles(jnp.stack([piece[:corner_rows] for piece in firsts]))
    corners = along_parts(corners)
    strips = along_tiles(jnp.stack([piece[corner_rows:] for piece in firsts]))
    teams = [
        [(z * ratio + c) * tile_count + t for z in range(groups) for t in range(tile_count)]
        for c in range(ratio)
    ]
    blocks = lax.all_to_all(main, both, 0, 0, tiled=True, axis_index_groups=teams)
    count = scen_count * tile_count
    scratch = [
        pltpu.VMEM((batch, block // 2 + 8, block), jnp.float32),
        pltpu.VMEM((batch * block, block), jnp.float32),
        pltpu.VMEM((batch * PIVOTS, block), jnp.float32),
        pltpu.VMEM((batch * PIVOTS, block), jnp.float32),
        zeros[0],
    ]
    inverse, background, plan, spots = pl.pallas_call(
        functools.partial(factor_kernel, batch, block, ratio, row_share),
        in_specs=[VMEM] * len(corners),
        out_specs=[VMEM, ANY, SMEM, SMEM],
        out_shape=[
            jax.ShapeDtypeStruct((batch * block, block), jnp.float32),
            jax.ShapeDtypeStruct((tall, wide), jnp.float32),
            jax.ShapeDtypeStruct((2, count), jnp.int32),
            jax.ShapeDtypeStruct((count + row_span,), jnp.int32),
        ],
        scratch_shapes=scratch + [
            pltpu.SMEM((count, groups), jnp.int32),
            pltpu.SMEM((row_span * group_size + 1,), jnp.int32),
            zeros[1],
        ],
        compiler_params=limit(*corners, *scratch),
    )(*corners)

    strips, inverse = lax.optimization_barrier((strips, inverse))
    strips = along_parts(strips)
    blocks, inverse = lax.optimization_barrier((blocks, inverse))
    blocks = along_parts([blocks])

    total = pltpu.VMEM((count + row_span, block, block), jnp.float32)
    schur = pl.pallas_call(
        functools.partial(scatter_kernel, block),
        in_specs=[SMEM, SMEM, VMEM] + [VMEM] * len(blocks) + [ANY],
        out_specs=ANY,
        out_shape=jax.ShapeDtypeStruct((tall, wide), jnp.float32),
        input_output_aliases={3 + len(blocks): 0},
        scratch_shapes=[total, pltpu.SemaphoreType.DMA((count + row_span,))],
        compiler_params=limit(*blocks, total),
    )(plan, spots, regular_rows, *blocks, background)
    strips, schur = lax.optimization_barrier((strips, schur))
    sums = [pltpu.VMEM((batch, row_share, block), jnp.float32)] * 2
    panel = pl.pallas_call(
        functools.partial(panel_kernel, batch, block),
        in_specs=[SMEM, VMEM, VMEM] + [VMEM] * len(strips),
        out_specs=ANY,
        out_shape=jax.ShapeDtypeStruct((row_share, batch * block), jnp.float32),
        scratch_shapes=sums + [pltpu.SemaphoreType.DMA((batch,))],
        compiler_params=limit(*strips, *sums),
    )(plan, regular_rows, inverse, *strips)
    return (schur, panel)


def solution(mesh):
    return jax.shard_map(
        local,
        mesh=mesh,
        in_specs=(
            P(("scen", "tile"), None, None),
            P(("scen", "tile"), None, None),
            P(("scen", "tile"), None),
            P(("scen", "tile")),
            P("scen"),
        ),
        out_specs=(P("scen", "tile"), P(("scen", "tile"), None)),
        check_vma=False,
    )
```

time: 112 us -> 67.6 us (0.60)
  waiting for transfers between devices: 32.6 us -> 12.5 us
  other arithmetic: 11.7 us -> 0.03 us
  starting transfers between devices: 31.6 us -> 23.2 us
  Pallas kernels: 29 us -> 25.7 us
  local copies, waits for them, and re-layouts: 5.04 us -> 3.58 us
    ppermute x6 -> x3, waiting for transfers between devices: 18.5 us -> 0.01 us  [along_place(): return lax.ppermute(array, 'scen', pairs)]
    select_n x1 -> x0, other arithmetic: 11.5 us -> none  [local(): background = jnp.where(row_id == col_id, regular[:, None], 0.0)]
    ppermute x6 -> x3, starting transfers between devices: 16.7 us -> 5.75 us  [along_place(): return lax.ppermute(array, 'scen', pairs)]
    ppermute x6, waiting for transfers between devices: 14.1 us -> 9.95 us  [along_tile(): return lax.ppermute(array, 'tile', [(t, t ^ k) for t in range(tile_count)])]
    pallas_call x4 -> x5, Pallas kernels: 29 us -> 25.7 us  [the longest x1 12.2 us: local(): pl.pallas_call(functools.partial(factor_kernel, batch, block, ratio, row_...]
    ppermute x3 -> x9, waiting for transfers between devices: 0.01 us -> 2.49 us  [along_part(): return lax.ppermute(array, 'scen', pairs)]
    another operation x0 -> x8, local copies, waits for them, and re-layouts: none -> 1.66 us  [the longest x4 0.87 us: local(): strips = along_tiles(jnp.stack([piece[corner_rows:] for piece in firsts]))]
    unnamed x17 -> x6, local copies, waits for them, and re-layouts: 3.4 us -> 1.92 us
  transfers between devices with their start and end apart: 16 -> 19, of which waited for: 4 -> 5; matrix products, arithmetic and copies ran while one was open for 15% -> 3% of each run, Pallas kernels for 14% -> 26%
where the time goes in v2:
time: 67.6 us; the launch traced here: 66.4 us
  Pallas kernels  25.7 us (38%)
  starting transfers between devices  23.2 us (34%)
  waiting for transfers between devices  12.5 us (18%)
  local copies, waits for them, and re-layouts  3.58 us (5%)
  between operations  1.47 us (2%)
    pallas_call x1, Pallas kernels, local(): pl.pallas_call(functools.partial(factor_kernel, batch, block, ratio, row_...  12.2 us
    ppermute x6, waiting for transfers between devices, along_tile(): return lax.ppermute(array, 'tile', [(t, t ^ k) for t in range(tile_count)])  9.95 us
    ppermute x6, starting transfers between devices, along_tile(): return lax.ppermute(array, 'tile', [(t, t ^ k) for t in range(tile_count)])  8.57 us
    all_to_all x1, starting transfers between devices, local(): lax.all_to_all(main, both, 0, 0, tiled=True, axis_index_groups=teams)  7.02 us
    ppermute x3, starting transfers between devices, along_place(): return lax.ppermute(array, 'scen', pairs)  5.75 us
    pallas_call x1, Pallas kernels, local(): pl.pallas_call(functools.partial(first_kernel, groups, block, group_size,...  5.21 us
    pallas_call x1, Pallas kernels, local(): pl.pallas_call(functools.partial(scatter_kernel, block), in_specs=[SMEM,...  3.51 us
    pallas_call x1, Pallas kernels, local(): pl.pallas_call(functools.partial(panel_kernel, batch, block), in_specs=[S...  3 us
  transfers between devices with their start and end apart: 19, of which 5 were waited for; matrix products, arithmetic and copies ran while one was open for 3% of the time, Pallas kernels for 26%

profile of v2, /device:TPU:0, one launch (start us, length us, event | category | flops | bytes accessed | tf_op | source)
XLA Modules:
  0.0 66.4 jit_solution(9429974904777609367)
XLA Ops:
  1.3 5.2 %shard_map.68 = (bf16[1024,512]{1,0:T(8,128)(2,1)}, f32[208,128]{1,0:T(8,128)}, f32[208,128]{1,0:T(8,128)}, f32[208,128]{1,0:T(8,128)}, f32[208,128]{1,0:T(8,128)}) custom-call(s32[1,4]{1,0:T(1,128)} %touched_ref.1, s32[1]{0:T(128)S(6)} %copy.9.live_ref, f32[16,128]{1,0:T(8,128)} %bitcast.19, bf16[1024,1024]{1,0:T(8,128)(2,1)} %bitcast.22, ...), custom_call_target="tpu_custom_call" | custom-call | tf_op jit(solution)/shard_map/pallas_call | solution.py:386
  6.5 5.1 %collective-permute-start.2 = (f32[208,128]{1,0:T(8,128)}, f32[208,128]{1,0:T(8,128)S(1)}, u32[]{:S(2)}, u32[]{:S(2)}) collective-permute-start(f32[208,128]{1,0:T(8,128)} %get-tuple-element.30), channel_id=1, source_target_pairs={{0,24},{4,28},{8,16},{12,20},{16,8},{20,12},{24,0},{28,4},{1,25},{... | collective-permute-start | bytes 319496 | tf_op jit(solution)/shard_map/ppermute | solution.py:410
  11.6 0.0 collective-permute-start.1
  11.6 0.6 collective-permute-start
  12.2 0.0 copy-start
  12.2 1.2 %copy-done = bf16[1024,512]{1,0:T(8,128)(2,1)S(1)} copy-done((bf16[1024,512]{1,0:T(8,128)(2,1)S(1)}, bf16[1024,512]{1,0:T(8,128)(2,1)}, u32[]{:S(2)}) %copy-start) | copy-done | bytes 1048600
  13.5 1.7 %shard_map.70 = f32[16,128,128]{2,1,0:T(8,128)} custom-call(bf16[1024,512]{1,0:T(8,128)(2,1)S(1)} %copy-done), custom_call_target="tpu_custom_call" | custom-call | tf_op jit(solution)/shard_map/pallas_call | solution.py:401
  15.2 7.0 %all-to-all-start = ((f32[16,128,128]{2,1,0:T(8,128)}), f32[16,128,128]{2,1,0:T(8,128)S(1)}, u32[]{:S(2)}, u32[]{:S(2)}) async-start(f32[16,128,128]{2,1,0:T(8,128)} %shard_map.70), calls=%async_computation | async-start | bytes 2097152 | tf_op jit(solution)/shard_map/all_to_all | solution.py:433
  22.2 0.8 %slice_bitcast_fusion.3 = f32[1,128,128]{2,1,0:T(8,128)S(1)} fusion(f32[208,128]{1,0:T(8,128)} %get-tuple-element.27), kind=kLoop, calls=%fused_computation.5 | loop fusion | bytes 131072 | tf_op jit(solution)/shard_map/stack | solution.py:428
  23.0 0.8 %slice_bitcast_fusion.7 = f32[1,80,128]{2,1,0:T(8,128)S(1)} fusion(f32[208,128]{1,0:T(8,128)} %get-tuple-element.27), kind=kLoop, calls=%fused_computation.9 | loop fusion | bytes 81920 | tf_op jit(solution)/shard_map/stack | solution.py:426
  23.8 0.0 collective-permute-done.2
  23.8 0.0 collective-permute-done.1
  23.9 0.0 collective-permute-done
  23.9 2.0 %collective-permute-start.6 = (f32[4,80,128]{2,1,0:T(8,128)S(1)}, f32[4,80,128]{2,1,0:T(8,128)S(1)}, u32[]{:S(2)}, u32[]{:S(2)}) collective-permute-start(f32[4,80,128]{2,1,0:T(8,128)S(1)} %pad_maximum_fusion.1.refs_0_), channel_id=1, source_target_pairs={{0,1},{1,0},{2,3},{3,2},{4,5},{5,4},{6,7},{7,6},{8,9},{9,8},{10,11... | collective-permute-start | bytes 491528 | tf_op jit(solution)/shard_map/ppermute | solution.py:413
  25.9 1.5 %collective-permute-start.7 = (f32[4,80,128]{2,1,0:T(8,128)S(1)}, f32[4,80,128]{2,1,0:T(8,128)S(1)}, u32[]{:S(2)}, u32[]{:S(2)}) collective-permute-start(f32[4,80,128]{2,1,0:T(8,128)S(1)} %pad_maximum_fusion.1.refs_0_), channel_id=1, source_target_pairs={{0,2},{1,3},{2,0},{3,1},{4,6},{5,7},{6,4},{7,5},{8,10},{9,11},{10,... | collective-permute-start | bytes 491528 | tf_op jit(solution)/shard_map/ppermute | solution.py:413
  27.4 0.1 collective-permute-start.8
  27.5 0.0 collective-permute-start.9
  27.5 5.2 %collective-permute-done.6.refs_1_ = f32[4,80,128]{2,1,0:T(8,128)S(1)} collective-permute-done((f32[4,80,128]{2,1,0:T(8,128)S(1)}, f32[4,80,128]{2,1,0:T(8,128)S(1)}, u32[]{:S(2)}, u32[]{:S(2)}) %collective-permute-start.6) | collective-permute-done | bytes 163872 | tf_op jit(solution)/shard_map/ppermute | solution.py:413
  32.7 0.0 collective-permute-start.10
  32.7 1.2 %collective-permute-start.3 = (f32[4,128,128]{2,1,0:T(8,128)S(1)}, f32[4,128,128]{2,1,0:T(8,128)S(1)}, u32[]{:S(2)}, u32[]{:S(2)}) collective-permute-start(f32[4,128,128]{2,1,0:T(8,128)S(1)} %pad_maximum_fusion.refs_0_), channel_id=1, source_target_pairs={{0,1},{1,0},{2,3},{3,2},{4,5},{5,4},{6,7},{7,6},{8,9},{9,8},{10,11... | collective-permute-start | bytes 786440 | tf_op jit(solution)/shard_map/ppermute | solution.py:413
  33.9 4.7 %collective-permute-done.7.refs_2_ = f32[4,80,128]{2,1,0:T(8,128)S(1)} collective-permute-done((f32[4,80,128]{2,1,0:T(8,128)S(1)}, f32[4,80,128]{2,1,0:T(8,128)S(1)}, u32[]{:S(2)}, u32[]{:S(2)}) %collective-permute-start.7) | collective-permute-done | bytes 163872 | tf_op jit(solution)/shard_map/ppermute | solution.py:413
  38.6 2.8 %collective-permute-start.4 = (f32[4,128,128]{2,1,0:T(8,128)S(1)}, f32[4,128,128]{2,1,0:T(8,128)S(1)}, u32[]{:S(2)}, u32[]{:S(2)}) collective-permute-start(f32[4,128,128]{2,1,0:T(8,128)S(1)} %pad_maximum_fusion.refs_0_), channel_id=1, source_target_pairs={{0,2},{1,3},{2,0},{3,1},{4,6},{5,7},{6,4},{7,5},{8,10},{9,11},{10,... | collective-permute-start | bytes 786440 | tf_op jit(solution)/shard_map/ppermute | solution.py:413
  41.5 0.0 collective-permute-done.8.refs_3_
  41.5 1.0 %collective-permute-start.5 = (f32[4,128,128]{2,1,0:T(8,128)S(1)}, f32[4,128,128]{2,1,0:T(8,128)S(1)}, u32[]{:S(2)}, u32[]{:S(2)}) collective-permute-start(f32[4,128,128]{2,1,0:T(8,128)S(1)} %pad_maximum_fusion.refs_0_), channel_id=1, source_target_pairs={{0,3},{1,2},{2,1},{3,0},{4,7},{5,6},{6,5},{7,4},{8,11},{9,10},{10,... | collective-permute-start | bytes 786440 | tf_op jit(solution)/shard_map/ppermute | solution.py:413
  42.5 0.0 collective-permute-done.9.refs_4_
  42.5 0.0 collective-permute-start.11
  42.5 0.0 collective-permute-done.10.refs_5_
  42.5 0.5 collective-permute-start.12
  43.0 0.9 %collective-permute-done.11.refs_6_ = f32[4,80,128]{2,1,0:T(8,128)S(1)} collective-permute-done((f32[4,80,128]{2,1,0:T(8,128)S(1)}, f32[4,80,128]{2,1,0:T(8,128)S(1)}, u32[]{:S(2)}, u32[]{:S(2)}) %collective-permute-start.11) | collective-permute-done | bytes 163872 | tf_op jit(solution)/shard_map/ppermute | solution.py:417
  43.9 0.2 collective-permute-done.12.refs_7_
  44.1 12.2 %shard_map.69 = (f32[1024,128]{1,0:T(8,128)S(1)}, f32[2048,4096]{1,0:T(8,128)}, s32[2,32]{1,0:T(2,128)S(1)}, s32[48]{0:T(128)S(1)}) custom-call(f32[4,80,128]{2,1,0:T(8,128)S(1)} %pad_maximum_fusion.1.refs_0_, f32[4,80,128]{2,1,0:T(8,128)S(1)} %collective-permute-done.6.refs_1_, f32[4,80,128]{2,1,0:T(8,128)S(1)} %collective-permute-done.7.refs_2_, ...), custom_call_target="tpu_custom_call" | custom-call | tf_op jit(solution)/shard_map/pallas_call | solution.py:442
  56.4 0.0 collective-permute-done.3.refs_1_
  56.4 0.0 collective-permute-done.4.refs_2_
  56.4 0.0 collective-permute-done.5.refs_3_
  56.4 0.0 all-to-all-done.refs_0_
  56.4 0.3 collective-permute-start.17
  56.8 0.2 collective-permute-start.13
  57.0 0.3 collective-permute-start.14
  57.3 0.2 collective-permute-start.15
  57.5 0.3 collective-permute-start.16
  57.8 1.4 %collective-permute-done.17.refs_1_ = f32[16,128,128]{2,1,0:T(8,128)S(1)} collective-permute-done((f32[16,128,128]{2,1,0:T(8,128)S(1)}, f32[16,128,128]{2,1,0:T(8,128)S(1)}, u32[]{:S(2)}, u32[]{:S(2)}) %collective-permute-start.17) | collective-permute-done | bytes 1048608 | tf_op jit(solution)/shard_map/ppermute | solution.py:417
  59.1 0.0 copy-start.1
  59.1 0.7 %copy-done.1 = f32[2048]{0:T(1024)S(1)} copy-done((f32[2048]{0:T(1024)S(1)}, f32[2048]{0:T(1024)}, u32[]{:S(2)}) %copy-start.1) | copy-done | bytes 8216
  59.8 0.0 copy-start.2
  59.8 3.5 %shard_map.71 = f32[2048,4096]{1,0:T(8,128)} custom-call(s32[2,32]{1,0:T(2,128)S(1)} %get-tuple-element.36.plan_ref, s32[48]{0:T(128)S(1)} %get-tuple-element.37.spot_ref, f32[16,128]{1,0:T(8,128)S(1)} %bitcast.20, f32[16,128,128]{2,1,0:T(8,128)S(1)} %all-to-all-done.refs_0_, ...), custom_call_target="tpu_custom_call", output_to_operand_aliasing={{}: (5, {})} | custom-call | tf_op jit(solution)/shard_map/pallas_call | solution.py:466
  63.4 0.0 collective-permute-done.13.refs_4_
  63.4 0.0 collective-permute-done.14.refs_5_
  63.4 0.0 collective-permute-done.15.refs_6_
  63.4 0.0 collective-permute-done.16.refs_7_
  63.4 0.0 copy-done.2
  63.4 3.0 %shard_map.72 = f32[512,1024]{1,0:T(8,128)} custom-call(s32[2,32]{1,0:T(2,128)S(1)} %get-tuple-element.36.plan_ref, f32[16,128]{1,0:T(8,128)S(1)} %bitcast.21, f32[1024,128]{1,0:T(8,128)S(1)} %get-tuple-element.43.inverse_ref, f32[4,128,128]{2,1,0:T(8,128)S(1)} %pad_maximum_fusion.refs_0_, f32[4,128,128]{2,1,0:T(8,128)S(1)} %collective-permute-done.3.refs_1_, ...), custom_call_target="tpu_custom_call" | custom-call | tf_op jit(solution)/shard_map/pallas_call | solution.py:477
  (8 shorter events, 0.1 us)
Async XLA Ops:
  6.5 17.3 %collective-permute-start.2 = (f32[208,128]{1,0:T(8,128)}, f32[208,128]{1,0:T(8,128)S(1)}, u32[]{:S(2)}, u32[]{:S(2)}) collective-permute-start(f32[208,128]{1,0:T(8,128)} %get-tuple-element.30), channel_id=1, source_target_pairs={{0,24},{4,28},{8,16},{12,20},{16,8},{20,12},{24,0},{28,4},{1,25},{... | collective-permute-start | bytes 319496 | tf_op jit(solution)/shard_map/ppermute | solution.py:410
  11.6 12.2 %collective-permute-start.1 = (f32[208,128]{1,0:T(8,128)}, f32[208,128]{1,0:T(8,128)S(1)}, u32[]{:S(2)}, u32[]{:S(2)}) collective-permute-start(f32[208,128]{1,0:T(8,128)} %get-tuple-element.29), channel_id=1, source_target_pairs={{0,16},{4,20},{8,24},{12,28},{16,0},{20,4},{24,8},{28,12},{1,17},{... | collective-permute-start | bytes 319496 | tf_op jit(solution)/shard_map/ppermute | solution.py:410
  11.6 12.3 %collective-permute-start = (f32[208,128]{1,0:T(8,128)}, f32[208,128]{1,0:T(8,128)S(1)}, u32[]{:S(2)}, u32[]{:S(2)}) collective-permute-start(f32[208,128]{1,0:T(8,128)} %get-tuple-element.28), channel_id=1, source_target_pairs={{0,8},{4,12},{8,0},{12,4},{16,24},{20,28},{24,16},{28,20},{1,9},{5... | collective-permute-start | bytes 319496 | tf_op jit(solution)/shard_map/ppermute | solution.py:410
  12.2 1.2 %copy-start = (bf16[1024,512]{1,0:T(8,128)(2,1)S(1)}, bf16[1024,512]{1,0:T(8,128)(2,1)}, u32[]{:S(2)}) copy-start(bf16[1024,512]{1,0:T(8,128)(2,1)} %get-tuple-element.38.scaled_ref) | copy-start | bytes 3145732
  15.2 41.2 %all-to-all-start = ((f32[16,128,128]{2,1,0:T(8,128)}), f32[16,128,128]{2,1,0:T(8,128)S(1)}, u32[]{:S(2)}, u32[]{:S(2)}) async-start(f32[16,128,128]{2,1,0:T(8,128)} %shard_map.70), calls=%async_computation | async-start | bytes 2097152 | tf_op jit(solution)/shard_map/all_to_all | solution.py:433
  23.9 8.8 %collective-permute-start.6 = (f32[4,80,128]{2,1,0:T(8,128)S(1)}, f32[4,80,128]{2,1,0:T(8,128)S(1)}, u32[]{:S(2)}, u32[]{:S(2)}) collective-permute-start(f32[4,80,128]{2,1,0:T(8,128)S(1)} %pad_maximum_fusion.1.refs_0_), channel_id=1, source_target_pairs={{0,1},{1,0},{2,3},{3,2},{4,5},{5,4},{6,7},{7,6},{8,9},{9,8},{10,11... | collective-permute-start | bytes 491528 | tf_op jit(solution)/shard_map/ppermute | solution.py:413
  25.9 12.7 %collective-permute-start.7 = (f32[4,80,128]{2,1,0:T(8,128)S(1)}, f32[4,80,128]{2,1,0:T(8,128)S(1)}, u32[]{:S(2)}, u32[]{:S(2)}) collective-permute-start(f32[4,80,128]{2,1,0:T(8,128)S(1)} %pad_maximum_fusion.1.refs_0_), channel_id=1, source_target_pairs={{0,2},{1,3},{2,0},{3,1},{4,6},{5,7},{6,4},{7,5},{8,10},{9,11},{10,... | collective-permute-start | bytes 491528 | tf_op jit(solution)/shard_map/ppermute | solution.py:413
  27.4 14.1 %collective-permute-start.8 = (f32[4,80,128]{2,1,0:T(8,128)S(1)}, f32[4,80,128]{2,1,0:T(8,128)S(1)}, u32[]{:S(2)}, u32[]{:S(2)}) collective-permute-start(f32[4,80,128]{2,1,0:T(8,128)S(1)} %pad_maximum_fusion.1.refs_0_), channel_id=1, source_target_pairs={{0,3},{1,2},{2,1},{3,0},{4,7},{5,6},{6,5},{7,4},{8,11},{9,10},{10,... | collective-permute-start | bytes 491528 | tf_op jit(solution)/shard_map/ppermute | solution.py:413
  27.5 15.0 %collective-permute-start.9 = (f32[4,80,128]{2,1,0:T(8,128)S(1)}, f32[4,80,128]{2,1,0:T(8,128)S(1)}, u32[]{:S(2)}, u32[]{:S(2)}) collective-permute-start(f32[4,80,128]{2,1,0:T(8,128)S(1)} %pad_maximum_fusion.1.refs_0_), channel_id=1, source_target_pairs={{0,4},{4,0},{8,12},{12,8},{16,20},{20,16},{24,28},{28,24},{1,5},{5... | collective-permute-start | bytes 491528 | tf_op jit(solution)/shard_map/ppermute | solution.py:417
  32.7 9.8 %collective-permute-start.10 = (f32[4,80,128]{2,1,0:T(8,128)S(1)}, f32[4,80,128]{2,1,0:T(8,128)S(1)}, u32[]{:S(2)}, u32[]{:S(2)}) collective-permute-start(f32[4,80,128]{2,1,0:T(8,128)S(1)} %collective-permute-done.6.refs_1_), channel_id=1, source_target_pairs={{0,4},{4,0},{8,12},{12,8},{16,20},{20,16},{24,28},{28,24},{1,5},{5... | collective-permute-start | bytes 491528 | tf_op jit(solution)/shard_map/ppermute | solution.py:417
  32.7 23.6 %collective-permute-start.3 = (f32[4,128,128]{2,1,0:T(8,128)S(1)}, f32[4,128,128]{2,1,0:T(8,128)S(1)}, u32[]{:S(2)}, u32[]{:S(2)}) collective-permute-start(f32[4,128,128]{2,1,0:T(8,128)S(1)} %pad_maximum_fusion.refs_0_), channel_id=1, source_target_pairs={{0,1},{1,0},{2,3},{3,2},{4,5},{5,4},{6,7},{7,6},{8,9},{9,8},{10,11... | collective-permute-start | bytes 786440 | tf_op jit(solution)/shard_map/ppermute | solution.py:413
  38.6 17.7 %collective-permute-start.4 = (f32[4,128,128]{2,1,0:T(8,128)S(1)}, f32[4,128,128]{2,1,0:T(8,128)S(1)}, u32[]{:S(2)}, u32[]{:S(2)}) collective-permute-start(f32[4,128,128]{2,1,0:T(8,128)S(1)} %pad_maximum_fusion.refs_0_), channel_id=1, source_target_pairs={{0,2},{1,3},{2,0},{3,1},{4,6},{5,7},{6,4},{7,5},{8,10},{9,11},{10,... | collective-permute-start | bytes 786440 | tf_op jit(solution)/shard_map/ppermute | solution.py:413
  41.5 14.9 %collective-permute-start.5 = (f32[4,128,128]{2,1,0:T(8,128)S(1)}, f32[4,128,128]{2,1,0:T(8,128)S(1)}, u32[]{:S(2)}, u32[]{:S(2)}) collective-permute-start(f32[4,128,128]{2,1,0:T(8,128)S(1)} %pad_maximum_fusion.refs_0_), channel_id=1, source_target_pairs={{0,3},{1,2},{2,1},{3,0},{4,7},{5,6},{6,5},{7,4},{8,11},{9,10},{10,... | collective-permute-start | bytes 786440 | tf_op jit(solution)/shard_map/ppermute | solution.py:413
  42.5 1.4 %collective-permute-start.11 = (f32[4,80,128]{2,1,0:T(8,128)S(1)}, f32[4,80,128]{2,1,0:T(8,128)S(1)}, u32[]{:S(2)}, u32[]{:S(2)}) collective-permute-start(f32[4,80,128]{2,1,0:T(8,128)S(1)} %collective-permute-done.7.refs_2_), channel_id=1, source_target_pairs={{0,4},{4,0},{8,12},{12,8},{16,20},{20,16},{24,28},{28,24},{1,5},{5... | collective-permute-start | bytes 491528 | tf_op jit(solution)/shard_map/ppermute | solution.py:417
  42.5 1.6 %collective-permute-start.12 = (f32[4,80,128]{2,1,0:T(8,128)S(1)}, f32[4,80,128]{2,1,0:T(8,128)S(1)}, u32[]{:S(2)}, u32[]{:S(2)}) collective-permute-start(f32[4,80,128]{2,1,0:T(8,128)S(1)} %collective-permute-done.8.refs_3_), channel_id=1, source_target_pairs={{0,4},{4,0},{8,12},{12,8},{16,20},{20,16},{24,28},{28,24},{1,5},{5... | collective-permute-start | bytes 491528 | tf_op jit(solution)/shard_map/ppermute | solution.py:417
  56.4 2.7 %collective-permute-start.17 = (f32[16,128,128]{2,1,0:T(8,128)S(1)}, f32[16,128,128]{2,1,0:T(8,128)S(1)}, u32[]{:S(2)}, u32[]{:S(2)}) collective-permute-start(f32[16,128,128]{2,1,0:T(8,128)S(1)} %all-to-all-done.refs_0_), channel_id=1, source_target_pairs={{0,4},{4,0},{8,12},{12,8},{16,20},{20,16},{24,28},{28,24},{1,5},{5... | collective-permute-start | bytes 3145736 | tf_op jit(solution)/shard_map/ppermute | solution.py:417
  56.8 6.6 %collective-permute-start.13 = (f32[4,128,128]{2,1,0:T(8,128)S(1)}, f32[4,128,128]{2,1,0:T(8,128)S(1)}, u32[]{:S(2)}, u32[]{:S(2)}) collective-permute-start(f32[4,128,128]{2,1,0:T(8,128)S(1)} %pad_maximum_fusion.refs_0_), channel_id=1, source_target_pairs={{0,4},{4,0},{8,12},{12,8},{16,20},{20,16},{24,28},{28,24},{1,5},{5... | collective-permute-start | bytes 786440 | tf_op jit(solution)/shard_map/ppermute | solution.py:417
  57.0 6.4 %collective-permute-start.14 = (f32[4,128,128]{2,1,0:T(8,128)S(1)}, f32[4,128,128]{2,1,0:T(8,128)S(1)}, u32[]{:S(2)}, u32[]{:S(2)}) collective-permute-start(f32[4,128,128]{2,1,0:T(8,128)S(1)} %collective-permute-done.3.refs_1_), channel_id=1, source_target_pairs={{0,4},{4,0},{8,12},{12,8},{16,20},{20,16},{24,28},{28,24},{1,5},{5... | collective-permute-start | bytes 786440 | tf_op jit(solution)/shard_map/ppermute | solution.py:417
  57.3 6.1 %collective-permute-start.15 = (f32[4,128,128]{2,1,0:T(8,128)S(1)}, f32[4,128,128]{2,1,0:T(8,128)S(1)}, u32[]{:S(2)}, u32[]{:S(2)}) collective-permute-start(f32[4,128,128]{2,1,0:T(8,128)S(1)} %collective-permute-done.4.refs_2_), channel_id=1, source_target_pairs={{0,4},{4,0},{8,12},{12,8},{16,20},{20,16},{24,28},{28,24},{1,5},{5... | collective-permute-start | bytes 786440 | tf_op jit(solution)/shard_map/ppermute | solution.py:417
  57.5 5.9 %collective-permute-start.16 = (f32[4,128,128]{2,1,0:T(8,128)S(1)}, f32[4,128,128]{2,1,0:T(8,128)S(1)}, u32[]{:S(2)}, u32[]{:S(2)}) collective-permute-start(f32[4,128,128]{2,1,0:T(8,128)S(1)} %collective-permute-done.5.refs_3_), channel_id=1, source_target_pairs={{0,4},{4,0},{8,12},{12,8},{16,20},{20,16},{24,28},{28,24},{1,5},{5... | collective-permute-start | bytes 786440 | tf_op jit(solution)/shard_map/ppermute | solution.py:417
  59.1 0.7 %copy-start.1 = (f32[2048]{0:T(1024)S(1)}, f32[2048]{0:T(1024)}, u32[]{:S(2)}) copy-start(f32[2048]{0:T(1024)} %param.9) | copy-start | bytes 24580
  59.8 3.6 %copy-start.2 = (f32[2048]{0:T(1024)S(1)}, f32[2048]{0:T(1024)}, u32[]{:S(2)}) copy-start(f32[2048]{0:T(1024)} %param.9) | copy-start | bytes 24580

commit v3 on v2

--- a/solution.py
+++ b/solution.py
@@ -12,6 +12,7 @@
 PANEL = 1024
 PIVOTS = 8
 ZEROS = 64
+EARLY = 0.375
 MIB = 1 << 20
 
 SMEM = pl.BlockSpec(memory_space=pltpu.SMEM)
@@ -24,12 +25,12 @@
     return lax.dot_general(left, right, (((0,), (0,)), ((), ())), preferred_element_type=jnp.float32)
 
 
-def fill(zero_scr, back_ref, sems):
+def fill(zero_scr, back_ref, sems, first, last):
     tall = zero_scr.shape[0]
     zero_scr[...] = jnp.zeros_like(zero_scr)
     copies = [
         pltpu.make_async_copy(zero_scr, back_ref.at[i * tall:(i + 1) * tall], sems.at[i])
-        for i in range(back_ref.shape[0] // tall)
+        for i in range(first, last)
     ]
     for copy in copies:
         copy.start()
@@ -38,9 +39,9 @@
 
 def first_kernel(
     groups, block, group_size, ratio, touched_ref, live_ref, regular_ref, inv_ref, border_ref,
-    scaled_ref, *refs,
+    main_ref, *refs,
 ):
-    *first_refs, inv_scr, border_scr, column_scr, inv_sem, border_sems = refs
+    *first_refs, scaled_ref, inv_scr, border_scr, column_scr, inv_sem, border_sems = refs
     place = lax.axis_index("scen") // ratio
     copies = []
     keeps, labels = [], []
@@ -81,13 +82,16 @@
         first_refs[k][half:half + 8] = last
         first_refs[k][half + 8:corner_rows] = root_rows
         first_refs[k][corner_rows:] = column_scr[place ^ k]
-
-
-def main_kernel(groups, block, scaled_ref, main_ref):
     for group in range(groups):
-        strip = gram(scaled_ref[:, group * block:(group + 1) * block], scaled_ref[...])
+        if group > 0:
+            strip = gram(scaled_ref[:, group * block:(group + 1) * block], scaled_ref[...])
         for other in range(groups):
             main_ref[group * groups + other] = strip[:, other * block:(other + 1) * block]
+
+
+def fill_kernel(early, after_ref, back_ref, zero_scr, sems):
+    for copy in fill(zero_scr, back_ref, sems, 0, early):
+        copy.wait()
 
 
 def pack_corner(groups, whole):
@@ -145,8 +149,8 @@
     return high, middle, rest - middle
 
 
-def factor_kernel(batch, block, ratio, share, *refs):
-    (*piece_refs, out_ref, back_ref, plan_ref, spot_ref,
+def factor_kernel(batch, block, ratio, share, early, *refs):
+    (*piece_refs, in_ref, out_ref, back_ref, plan_ref, spot_ref,
      packed_scr, sum_scr, mult_scr, pivot_scr, zero_scr, label_scr, owner_scr, sems) = refs
     half = block // 2
     scen, tile = lax.axis_index("scen"), lax.axis_index("tile")
@@ -176,7 +180,7 @@
         wanted = wanted & (row < device_row + share) & (device_row < row + block)
         plan_ref[1, i] = jnp.where(wanted, jnp.maximum(row - device_row, 0) // block * batch + column, -1)
 
-    copies = fill(zero_scr, back_ref, sems)
+    copies = fill(zero_scr, back_ref, sems, early, back_ref.shape[0] // zero_scr.shape[0])
     for i in range(nowhere + 1):
         owner_scr[i] = -1
     for i in range(tall):
@@ -381,15 +385,17 @@
     regular_rows = regular.reshape(-1, block)
 
     tall, wide = row_span * block, group_size * block
+    early = int(tall // ZEROS * EARLY)
     zeros = [pltpu.VMEM((ZEROS, wide), jnp.float32), pltpu.SemaphoreType.DMA((tall // ZEROS,))]
 
-    scaled, *first = pl.pallas_call(
+    main, *first = pl.pallas_call(
         functools.partial(first_kernel, groups, block, group_size, ratio),
         in_specs=[SMEM, SMEM, VMEM, HBM, HBM],
         out_specs=[VMEM] * (groups + 1),
-        out_shape=[jax.ShapeDtypeStruct((order_size, width), border.dtype)]
+        out_shape=[jax.ShapeDtypeStruct((groups * groups, block, block), jnp.float32)]
         + [jax.ShapeDtypeStruct((corner_rows + block, block), jnp.float32)] * groups,
         scratch_shapes=[
+            pltpu.VMEM((order_size, width), border.dtype),
             pltpu.VMEM((order_size, order_size), inv_factor.dtype),
             pltpu.VMEM((order_size, width), border.dtype),
             pltpu.VMEM((groups, block, block), jnp.float32),
@@ -398,13 +404,6 @@
         ],
         compiler_params=pltpu.CompilerParams(vmem_limit_bytes=60 * MIB),
     )(touched, live_count, regular_rows, inv_factor[0], border[0])
-    main = pl.pallas_call(
-        functools.partial(main_kernel, groups, block),
-        in_specs=[VMEM],
-        out_specs=VMEM,
-        out_shape=jax.ShapeDtypeStruct((groups * groups, block, block), jnp.float32),
-        compiler_params=limit(scaled, jax.ShapeDtypeStruct((groups * groups, block, block), jnp.float32)),
-    )(scaled)
     def along_place(array, k):
         pairs = [(s, (s // ratio ^ k) * ratio + s % ratio) for s in range(scen_count)]
         return lax.ppermute(array, "scen", pairs)
@@ -424,8 +423,19 @@
 
     firsts = [first[0]] + [along_place(first[k], k) for k in range(1, groups)]
     corners = along_tiles(jnp.stack([piece[:corner_rows] for piece in firsts]))
+    background = pl.pallas_call(
+        functools.partial(fill_kernel, early),
+        in_specs=[ANY],
+        out_specs=ANY,
+        out_shape=jax.ShapeDtypeStruct((tall, wide), jnp.float32),
+        scratch_shapes=zeros,
+        cost_estimate=pl.CostEstimate(flops=0, bytes_accessed=4 * early * ZEROS * wide, transcendentals=0),
+        compiler_params=limit(zeros[0]),
+    )(corners[1])
+    strip = jnp.stack([piece[corner_rows:] for piece in firsts])
+    later, background = lax.optimization_barrier((strip, background))
+    strips = [strip, along_tile(strip, 1)] + [along_tile(later, k) for k in range(2, tile_count)]
     corners = along_parts(corners)
-    strips = along_tiles(jnp.stack([piece[corner_rows:] for piece in firsts]))
     teams = [
         [(z * ratio + c) * tile_count + t for z in range(groups) for t in range(tile_count)]
         for c in range(ratio)
@@ -440,8 +450,9 @@
         zeros[0],
     ]
     inverse, background, plan, spots = pl.pallas_call(
-        functools.partial(factor_kernel, batch, block, ratio, row_share),
-        in_specs=[VMEM] * len(corners),
+        functools.partial(factor_kernel, batch, block, ratio, row_share, early),
+        in_specs=[VMEM] * len(corners) + [ANY],
+        input_output_aliases={len(corners): 1},
         out_specs=[VMEM, ANY, SMEM, SMEM],
         out_shape=[
             jax.ShapeDtypeStruct((batch * block, block), jnp.float32),
@@ -455,7 +466,7 @@
             zeros[1],
         ],
         compiler_params=limit(*corners, *scratch),
-    )(*corners)
+    )(*corners, background)
 
     strips, inverse = lax.optimization_barrier((strips, inverse))
     strips = along_parts(strips)

time: 67.6 us -> 64.1 us (0.948); the launches traced: 66.4 us -> 63.8 us
  waiting for transfers between devices: 12.5 us -> 8.67 us
  local copies, waits for them, and re-layouts: 3.58 us -> 1.67 us
  starting transfers between devices: 23.2 us -> 24.8 us
  Pallas kernels: 25.7 us -> 27.1 us
    ppermute x6, waiting for transfers between devices: 9.95 us -> 6.16 us  [along_tile(): return lax.ppermute(array, 'tile', [(t, t ^ k) for t in range(tile_count)])]
    pallas_call x1, Pallas kernels: 1.71 us -> 4.91 us  [local(): pl.pallas_call(functools.partial(fill_kernel, early), in_specs=[ANY], out...]
    pallas_call x1, Pallas kernels: 12.2 us -> 9.95 us  [local(): pl.pallas_call(functools.partial(factor_kernel, batch, block, ratio, row_...]
    unnamed x6 -> x2, local copies, waits for them, and re-layouts: 1.92 us -> 0.01 us
    ppermute x6, starting transfers between devices: 8.57 us -> 10.2 us  [along_tile(): return lax.ppermute(array, 'tile', [(t, t ^ k) for t in range(tile_count)])]
  transfers between devices with their start and end apart: 19 -> 19, of which waited for: 5 -> 5; matrix products, arithmetic and copies ran while one was open for 3% -> 3% of each run, Pallas kernels for 26% -> 29%
where the time goes in v3:
time: 64.1 us; the launch traced here: 63.8 us
  Pallas kernels  27.1 us (42%)
  starting transfers between devices  24.8 us (39%)
  waiting for transfers between devices  8.67 us (14%)
  local copies, waits for them, and re-layouts  1.67 us (3%)
  between operations  1.48 us (2%)
    ppermute x6, starting transfers between devices, along_tile(): return lax.ppermute(array, 'tile', [(t, t ^ k) for t in range(tile_count)])  10.2 us
    pallas_call x1, Pallas kernels, local(): pl.pallas_call(functools.partial(factor_kernel, batch, block, ratio, row_...  9.95 us
    all_to_all x1, starting transfers between devices, local(): lax.all_to_all(main, both, 0, 0, tiled=True, axis_index_groups=teams)  7.01 us
    ppermute x6, waiting for transfers between devices, along_tile(): return lax.ppermute(array, 'tile', [(t, t ^ k) for t in range(tile_count)])  6.16 us
    pallas_call x1, Pallas kernels, local(): pl.pallas_call(functools.partial(first_kernel, groups, block, group_size,...  5.76 us
    ppermute x3, starting transfers between devices, along_place(): return lax.ppermute(array, 'scen', pairs)  5.75 us
    pallas_call x1, Pallas kernels, local(): pl.pallas_call(functools.partial(fill_kernel, early), in_specs=[ANY], out...  4.91 us
    pallas_call x1, Pallas kernels, local(): pl.pallas_call(functools.partial(scatter_kernel, block), in_specs=[SMEM,...  3.49 us
  transfers between devices with their start and end apart: 19, of which 5 were waited for; matrix products, arithmetic and copies ran while one was open for 3% of the time, Pallas kernels for 29%

profile of v3, /device:TPU:0, one launch (start us, length us, event | category | flops | bytes accessed | tf_op | source)
XLA Modules:
  0.0 63.8 jit_solution(15708601383599644760)
XLA Ops:
  1.3 5.8 %shard_map.68 = (f32[16,128,128]{2,1,0:T(8,128)}, f32[208,128]{1,0:T(8,128)}, f32[208,128]{1,0:T(8,128)}, f32[208,128]{1,0:T(8,128)}, f32[208,128]{1,0:T(8,128)}) custom-call(s32[1,4]{1,0:T(1,128)} %touched_ref.1, s32[1]{0:T(128)S(6)} %copy.11.live_ref, f32[16,128]{1,0:T(8,128)} %bitcast.19, bf16[1024,1024]{1,0:T(8,128)(2,1)} %bitcast.22, ...), custom_call_target="tpu_custom_call" | custom-call | tf_op jit(solution)/shard_map/pallas_call | solution.py:391
  7.0 5.1 %collective-permute-start.2 = (f32[208,128]{1,0:T(8,128)}, f32[208,128]{1,0:T(8,128)S(1)}, u32[]{:S(2)}, u32[]{:S(2)}) collective-permute-start(f32[208,128]{1,0:T(8,128)} %get-tuple-element.32), channel_id=1, source_target_pairs={{0,24},{4,28},{8,16},{12,20},{16,8},{20,12},{24,0},{28,4},{1,25},{... | collective-permute-start | bytes 319496 | tf_op jit(solution)/shard_map/ppermute | solution.py:409
  12.2 0.0 collective-permute-start.1
  12.2 0.6 %collective-permute-start = (f32[208,128]{1,0:T(8,128)}, f32[208,128]{1,0:T(8,128)S(1)}, u32[]{:S(2)}, u32[]{:S(2)}) collective-permute-start(f32[208,128]{1,0:T(8,128)} %get-tuple-element.30), channel_id=1, source_target_pairs={{0,8},{4,12},{8,0},{12,4},{16,24},{20,28},{24,16},{28,20},{1,9},{5... | collective-permute-start | bytes 319496 | tf_op jit(solution)/shard_map/ppermute | solution.py:409
  12.8 7.0 %all-to-all-start = ((f32[16,128,128]{2,1,0:T(8,128)}), f32[16,128,128]{2,1,0:T(8,128)S(1)}, u32[]{:S(2)}, u32[]{:S(2)}) async-start(f32[16,128,128]{2,1,0:T(8,128)} %get-tuple-element.42), calls=%async_computation | async-start | bytes 2097152 | tf_op jit(solution)/shard_map/all_to_all | solution.py:443
  19.8 0.8 %slice_bitcast_fusion.3 = f32[1,128,128]{2,1,0:T(8,128)S(1)} fusion(f32[208,128]{1,0:T(8,128)} %get-tuple-element.29), kind=kLoop, calls=%fused_computation.5 | loop fusion | bytes 131072 | tf_op jit(solution)/shard_map/stack | solution.py:435
  20.7 0.8 %slice_bitcast_fusion.7 = f32[1,80,128]{2,1,0:T(8,128)S(1)} fusion(f32[208,128]{1,0:T(8,128)} %get-tuple-element.29), kind=kLoop, calls=%fused_computation.9 | loop fusion | bytes 81920 | tf_op jit(solution)/shard_map/stack | solution.py:425
  21.4 0.0 collective-permute-done.2
  21.5 0.0 collective-permute-done.1
  21.5 0.0 collective-permute-done
  21.5 2.0 %collective-permute-start.4 = (f32[4,80,128]{2,1,0:T(8,128)S(1)}, f32[4,80,128]{2,1,0:T(8,128)S(1)}, u32[]{:S(2)}, u32[]{:S(2)}) collective-permute-start(f32[4,80,128]{2,1,0:T(8,128)S(1)} %pad_maximum_fusion.1.refs_0_), channel_id=1, source_target_pairs={{0,1},{1,0},{2,3},{3,2},{4,5},{5,4},{6,7},{7,6},{8,9},{9,8},{10,11... | collective-permute-start | bytes 491528 | tf_op jit(solution)/shard_map/ppermute | solution.py:412
  23.5 1.5 %collective-permute-start.7 = (f32[4,80,128]{2,1,0:T(8,128)S(1)}, f32[4,80,128]{2,1,0:T(8,128)S(1)}, u32[]{:S(2)}, u32[]{:S(2)}) collective-permute-start(f32[4,80,128]{2,1,0:T(8,128)S(1)} %pad_maximum_fusion.1.refs_0_), channel_id=1, source_target_pairs={{0,2},{1,3},{2,0},{3,1},{4,6},{5,7},{6,4},{7,5},{8,10},{9,11},{10,... | collective-permute-start | bytes 491528 | tf_op jit(solution)/shard_map/ppermute | solution.py:412
  25.0 0.1 collective-permute-start.8
  25.1 0.0 collective-permute-start.9
  25.1 5.9 %collective-permute-done.4.after_ref.refs_1_ = f32[4,80,128]{2,1,0:T(8,128)S(1)} collective-permute-done((f32[4,80,128]{2,1,0:T(8,128)S(1)}, f32[4,80,128]{2,1,0:T(8,128)S(1)}, u32[]{:S(2)}, u32[]{:S(2)}) %collective-permute-start.4) | collective-permute-done | bytes 163872 | tf_op jit(solution)/shard_map/ppermute | solution.py:412
  31.0 0.0 collective-permute-start.10
  31.1 0.0 copy-start
  31.1 0.1 collective-permute-start.3
  31.1 4.9 %shard_map.69.refs_8_ = f32[2048,4096]{1,0:T(8,128)} custom-call(f32[4,80,128]{2,1,0:T(8,128)S(1)} %collective-permute-done.4.after_ref.refs_1_), custom_call_target="tpu_custom_call" | custom-call | bytes 12582912 | tf_op jit(solution)/shard_map/pallas_call | solution.py:426
  36.1 0.2 collective-permute-done.7.refs_2_
  36.3 5.4 %collective-permute-start.5 = (f32[4,128,128]{2,1,0:T(8,128)S(1)}, f32[4,128,128]{2,1,0:T(8,128)S(1)}, u32[]{:S(2)}, u32[]{:S(2)}) collective-permute-start(f32[4,128,128]{2,1,0:T(8,128)S(1)} %pad_maximum_fusion.refs_0_), channel_id=1, source_target_pairs={{0,2},{1,3},{2,0},{3,1},{4,6},{5,7},{6,4},{7,5},{8,10},{9,11},{10,... | collective-permute-start | bytes 786440 | tf_op jit(solution)/shard_map/ppermute | solution.py:412
  41.7 0.0 collective-permute-done.8.refs_3_
  41.7 1.2 %collective-permute-start.6 = (f32[4,128,128]{2,1,0:T(8,128)S(1)}, f32[4,128,128]{2,1,0:T(8,128)S(1)}, u32[]{:S(2)}, u32[]{:S(2)}) collective-permute-start(f32[4,128,128]{2,1,0:T(8,128)S(1)} %pad_maximum_fusion.refs_0_), channel_id=1, source_target_pairs={{0,3},{1,2},{2,1},{3,0},{4,7},{5,6},{6,5},{7,4},{8,11},{9,10},{10,... | collective-permute-start | bytes 786440 | tf_op jit(solution)/shard_map/ppermute | solution.py:412
  42.9 0.0 collective-permute-done.9.refs_4_
  42.9 0.0 collective-permute-start.11
  42.9 0.0 collective-permute-done.10.refs_5_
  42.9 0.5 collective-permute-start.12
  43.4 0.9 %collective-permute-done.11.refs_6_ = f32[4,80,128]{2,1,0:T(8,128)S(1)} collective-permute-done((f32[4,80,128]{2,1,0:T(8,128)S(1)}, f32[4,80,128]{2,1,0:T(8,128)S(1)}, u32[]{:S(2)}, u32[]{:S(2)}) %collective-permute-start.11) | collective-permute-done | bytes 163872 | tf_op jit(solution)/shard_map/ppermute | solution.py:416
  44.3 0.2 collective-permute-done.12.refs_7_
  44.5 10.0 %shard_map.70 = (f32[1024,128]{1,0:T(8,128)S(1)}, f32[2048,4096]{1,0:T(8,128)}, s32[2,32]{1,0:T(2,128)S(1)}, s32[48]{0:T(128)S(1)}) custom-call(f32[4,80,128]{2,1,0:T(8,128)S(1)} %pad_maximum_fusion.1.refs_0_, f32[4,80,128]{2,1,0:T(8,128)S(1)} %collective-permute-done.4.after_ref.refs_1_, ...), custom_call_target="tpu_custom_call", output_to_operand_aliasing={{1}: (8, {})} | custom-call | tf_op jit(solution)/shard_map/pallas_call | solution.py:452
  54.5 0.0 collective-permute-done.3.refs_1_
  54.5 0.0 collective-permute-done.5.refs_2_
  54.5 0.0 collective-permute-done.6.refs_3_
  54.5 0.0 all-to-all-done.refs_0_
  54.5 0.3 collective-permute-start.17
  54.8 0.2 collective-permute-start.13
  55.1 0.3 collective-permute-start.14
  55.4 0.2 collective-permute-start.15
  55.6 0.3 collective-permute-start.16
  55.9 1.4 %collective-permute-done.17.refs_1_ = f32[16,128,128]{2,1,0:T(8,128)S(1)} collective-permute-done((f32[16,128,128]{2,1,0:T(8,128)S(1)}, f32[16,128,128]{2,1,0:T(8,128)S(1)}, u32[]{:S(2)}, u32[]{:S(2)}) %collective-permute-start.17) | collective-permute-done | bytes 1048608 | tf_op jit(solution)/shard_map/ppermute | solution.py:416
  57.2 0.0 copy-done
  57.2 3.5 %shard_map.71 = f32[2048,4096]{1,0:T(8,128)} custom-call(s32[2,32]{1,0:T(2,128)S(1)} %get-tuple-element.40.plan_ref, s32[48]{0:T(128)S(1)} %get-tuple-element.41.spot_ref, f32[16,128]{1,0:T(8,128)S(1)} %bitcast.20, f32[16,128,128]{2,1,0:T(8,128)S(1)} %all-to-all-done.refs_0_, ...), custom_call_target="tpu_custom_call", output_to_operand_aliasing={{}: (5, {})} | custom-call | tf_op jit(solution)/shard_map/pallas_call | solution.py:477
  60.7 0.0 collective-permute-done.13.refs_4_
  60.7 0.0 collective-permute-done.14.refs_5_
  60.7 0.0 collective-permute-done.15.refs_6_
  60.8 0.0 collective-permute-done.16.refs_7_
  60.8 3.0 %shard_map.72 = f32[512,1024]{1,0:T(8,128)} custom-call(s32[2,32]{1,0:T(2,128)S(1)} %get-tuple-element.40.plan_ref, f32[16,128]{1,0:T(8,128)S(1)} %bitcast.21, f32[1024,128]{1,0:T(8,128)S(1)} %get-tuple-element.47.inverse_ref, f32[4,128,128]{2,1,0:T(8,128)S(1)} %pad_maximum_fusion.refs_0_, f32[4,128,128]{2,1,0:T(8,128)S(1)} %collective-permute-done.3.refs_1_, ...), custom_call_target="tpu_custom_call" | custom-call | tf_op jit(solution)/shard_map/pallas_call | solution.py:488
  (8 shorter events, 0.1 us)
Async XLA Ops:
  7.0 14.4 %collective-permute-start.2 = (f32[208,128]{1,0:T(8,128)}, f32[208,128]{1,0:T(8,128)S(1)}, u32[]{:S(2)}, u32[]{:S(2)}) collective-permute-start(f32[208,128]{1,0:T(8,128)} %get-tuple-element.32), channel_id=1, source_target_pairs={{0,24},{4,28},{8,16},{12,20},{16,8},{20,12},{24,0},{28,4},{1,25},{... | collective-permute-start | bytes 319496 | tf_op jit(solution)/shard_map/ppermute | solution.py:409
  12.2 9.3 %collective-permute-start.1 = (f32[208,128]{1,0:T(8,128)}, f32[208,128]{1,0:T(8,128)S(1)}, u32[]{:S(2)}, u32[]{:S(2)}) collective-permute-start(f32[208,128]{1,0:T(8,128)} %get-tuple-element.31), channel_id=1, source_target_pairs={{0,16},{4,20},{8,24},{12,28},{16,0},{20,4},{24,8},{28,12},{1,17},{... | collective-permute-start | bytes 319496 | tf_op jit(solution)/shard_map/ppermute | solution.py:409
  12.2 9.3 %collective-permute-start = (f32[208,128]{1,0:T(8,128)}, f32[208,128]{1,0:T(8,128)S(1)}, u32[]{:S(2)}, u32[]{:S(2)}) collective-permute-start(f32[208,128]{1,0:T(8,128)} %get-tuple-element.30), channel_id=1, source_target_pairs={{0,8},{4,12},{8,0},{12,4},{16,24},{20,28},{24,16},{28,20},{1,9},{5... | collective-permute-start | bytes 319496 | tf_op jit(solution)/shard_map/ppermute | solution.py:409
  12.8 41.7 %all-to-all-start = ((f32[16,128,128]{2,1,0:T(8,128)}), f32[16,128,128]{2,1,0:T(8,128)S(1)}, u32[]{:S(2)}, u32[]{:S(2)}) async-start(f32[16,128,128]{2,1,0:T(8,128)} %get-tuple-element.42), calls=%async_computation | async-start | bytes 2097152 | tf_op jit(solution)/shard_map/all_to_all | solution.py:443
  21.5 9.5 %collective-permute-start.4 = (f32[4,80,128]{2,1,0:T(8,128)S(1)}, f32[4,80,128]{2,1,0:T(8,128)S(1)}, u32[]{:S(2)}, u32[]{:S(2)}) collective-permute-start(f32[4,80,128]{2,1,0:T(8,128)S(1)} %pad_maximum_fusion.1.refs_0_), channel_id=1, source_target_pairs={{0,1},{1,0},{2,3},{3,2},{4,5},{5,4},{6,7},{7,6},{8,9},{9,8},{10,11... | collective-permute-start | bytes 491528 | tf_op jit(solution)/shard_map/ppermute | solution.py:412
  23.5 12.8 %collective-permute-start.7 = (f32[4,80,128]{2,1,0:T(8,128)S(1)}, f32[4,80,128]{2,1,0:T(8,128)S(1)}, u32[]{:S(2)}, u32[]{:S(2)}) collective-permute-start(f32[4,80,128]{2,1,0:T(8,128)S(1)} %pad_maximum_fusion.1.refs_0_), channel_id=1, source_target_pairs={{0,2},{1,3},{2,0},{3,1},{4,6},{5,7},{6,4},{7,5},{8,10},{9,11},{10,... | collective-permute-start | bytes 491528 | tf_op jit(solution)/shard_map/ppermute | solution.py:412
  25.0 16.7 %collective-permute-start.8 = (f32[4,80,128]{2,1,0:T(8,128)S(1)}, f32[4,80,128]{2,1,0:T(8,128)S(1)}, u32[]{:S(2)}, u32[]{:S(2)}) collective-permute-start(f32[4,80,128]{2,1,0:T(8,128)S(1)} %pad_maximum_fusion.1.refs_0_), channel_id=1, source_target_pairs={{0,3},{1,2},{2,1},{3,0},{4,7},{5,6},{6,5},{7,4},{8,11},{9,10},{10,... | collective-permute-start | bytes 491528 | tf_op jit(solution)/shard_map/ppermute | solution.py:412
  25.1 17.8 %collective-permute-start.9 = (f32[4,80,128]{2,1,0:T(8,128)S(1)}, f32[4,80,128]{2,1,0:T(8,128)S(1)}, u32[]{:S(2)}, u32[]{:S(2)}) collective-permute-start(f32[4,80,128]{2,1,0:T(8,128)S(1)} %pad_maximum_fusion.1.refs_0_), channel_id=1, source_target_pairs={{0,4},{4,0},{8,12},{12,8},{16,20},{20,16},{24,28},{28,24},{1,5},{5... | collective-permute-start | bytes 491528 | tf_op jit(solution)/shard_map/ppermute | solution.py:416
  31.0 11.9 %collective-permute-start.10 = (f32[4,80,128]{2,1,0:T(8,128)S(1)}, f32[4,80,128]{2,1,0:T(8,128)S(1)}, u32[]{:S(2)}, u32[]{:S(2)}) collective-permute-start(f32[4,80,128]{2,1,0:T(8,128)S(1)} %collective-permute-done.4.after_ref.refs_1_), channel_id=1, source_target_pairs={{0,4},{4,0},{8,12},{12,8},{16,20},{20,16},{24,28},{28,24},{1,5},{5... | collective-permute-start | bytes 491528 | tf_op jit(solution)/shard_map/ppermute | solution.py:416
  31.1 26.2 %copy-start = (f32[2048]{0:T(1024)S(1)}, f32[2048]{0:T(1024)}, u32[]{:S(2)}) copy-start(f32[2048]{0:T(1024)} %param.9) | copy-start | bytes 24580
  31.1 23.4 %collective-permute-start.3 = (f32[4,128,128]{2,1,0:T(8,128)S(1)}, f32[4,128,128]{2,1,0:T(8,128)S(1)}, u32[]{:S(2)}, u32[]{:S(2)}) collective-permute-start(f32[4,128,128]{2,1,0:T(8,128)S(1)} %pad_maximum_fusion.refs_0_), channel_id=1, source_target_pairs={{0,1},{1,0},{2,3},{3,2},{4,5},{5,4},{6,7},{7,6},{8,9},{9,8},{10,11... | collective-permute-start | bytes 786440 | tf_op jit(solution)/shard_map/ppermute | solution.py:412
  36.3 18.2 %collective-permute-start.5 = (f32[4,128,128]{2,1,0:T(8,128)S(1)}, f32[4,128,128]{2,1,0:T(8,128)S(1)}, u32[]{:S(2)}, u32[]{:S(2)}) collective-permute-start(f32[4,128,128]{2,1,0:T(8,128)S(1)} %pad_maximum_fusion.refs_0_), channel_id=1, source_target_pairs={{0,2},{1,3},{2,0},{3,1},{4,6},{5,7},{6,4},{7,5},{8,10},{9,11},{10,... | collective-permute-start | bytes 786440 | tf_op jit(solution)/shard_map/ppermute | solution.py:412
  41.7 12.8 %collective-permute-start.6 = (f32[4,128,128]{2,1,0:T(8,128)S(1)}, f32[4,128,128]{2,1,0:T(8,128)S(1)}, u32[]{:S(2)}, u32[]{:S(2)}) collective-permute-start(f32[4,128,128]{2,1,0:T(8,128)S(1)} %pad_maximum_fusion.refs_0_), channel_id=1, source_target_pairs={{0,3},{1,2},{2,1},{3,0},{4,7},{5,6},{6,5},{7,4},{8,11},{9,10},{10,... | collective-permute-start | bytes 786440 | tf_op jit(solution)/shard_map/ppermute | solution.py:412
  42.9 1.4 %collective-permute-start.11 = (f32[4,80,128]{2,1,0:T(8,128)S(1)}, f32[4,80,128]{2,1,0:T(8,128)S(1)}, u32[]{:S(2)}, u32[]{:S(2)}) collective-permute-start(f32[4,80,128]{2,1,0:T(8,128)S(1)} %collective-permute-done.7.refs_2_), channel_id=1, source_target_pairs={{0,4},{4,0},{8,12},{12,8},{16,20},{20,16},{24,28},{28,24},{1,5},{5... | collective-permute-start | bytes 491528 | tf_op jit(solution)/shard_map/ppermute | solution.py:416
  42.9 1.6 %collective-permute-start.12 = (f32[4,80,128]{2,1,0:T(8,128)S(1)}, f32[4,80,128]{2,1,0:T(8,128)S(1)}, u32[]{:S(2)}, u32[]{:S(2)}) collective-permute-start(f32[4,80,128]{2,1,0:T(8,128)S(1)} %collective-permute-done.8.refs_3_), channel_id=1, source_target_pairs={{0,4},{4,0},{8,12},{12,8},{16,20},{20,16},{24,28},{28,24},{1,5},{5... | collective-permute-start | bytes 491528 | tf_op jit(solution)/shard_map/ppermute | solution.py:416
  54.5 2.7 %collective-permute-start.17 = (f32[16,128,128]{2,1,0:T(8,128)S(1)}, f32[16,128,128]{2,1,0:T(8,128)S(1)}, u32[]{:S(2)}, u32[]{:S(2)}) collective-permute-start(f32[16,128,128]{2,1,0:T(8,128)S(1)} %all-to-all-done.refs_0_), channel_id=1, source_target_pairs={{0,4},{4,0},{8,12},{12,8},{16,20},{20,16},{24,28},{28,24},{1,5},{5... | collective-permute-start | bytes 3145736 | tf_op jit(solution)/shard_map/ppermute | solution.py:416
  54.8 5.9 %collective-permute-start.13 = (f32[4,128,128]{2,1,0:T(8,128)S(1)}, f32[4,128,128]{2,1,0:T(8,128)S(1)}, u32[]{:S(2)}, u32[]{:S(2)}) collective-permute-start(f32[4,128,128]{2,1,0:T(8,128)S(1)} %pad_maximum_fusion.refs_0_), channel_id=1, source_target_pairs={{0,4},{4,0},{8,12},{12,8},{16,20},{20,16},{24,28},{28,24},{1,5},{5... | collective-permute-start | bytes 786440 | tf_op jit(solution)/shard_map/ppermute | solution.py:416
  55.1 5.7 %collective-permute-start.14 = (f32[4,128,128]{2,1,0:T(8,128)S(1)}, f32[4,128,128]{2,1,0:T(8,128)S(1)}, u32[]{:S(2)}, u32[]{:S(2)}) collective-permute-start(f32[4,128,128]{2,1,0:T(8,128)S(1)} %collective-permute-done.3.refs_1_), channel_id=1, source_target_pairs={{0,4},{4,0},{8,12},{12,8},{16,20},{20,16},{24,28},{28,24},{1,5},{5... | collective-permute-start | bytes 786440 | tf_op jit(solution)/shard_map/ppermute | solution.py:416
  55.4 5.4 %collective-permute-start.15 = (f32[4,128,128]{2,1,0:T(8,128)S(1)}, f32[4,128,128]{2,1,0:T(8,128)S(1)}, u32[]{:S(2)}, u32[]{:S(2)}) collective-permute-start(f32[4,128,128]{2,1,0:T(8,128)S(1)} %collective-permute-done.5.refs_2_), channel_id=1, source_target_pairs={{0,4},{4,0},{8,12},{12,8},{16,20},{20,16},{24,28},{28,24},{1,5},{5... | collective-permute-start | bytes 786440 | tf_op jit(solution)/shard_map/ppermute | solution.py:416
  55.6 5.2 %collective-permute-start.16 = (f32[4,128,128]{2,1,0:T(8,128)S(1)}, f32[4,128,128]{2,1,0:T(8,128)S(1)}, u32[]{:S(2)}, u32[]{:S(2)}) collective-permute-start(f32[4,128,128]{2,1,0:T(8,128)S(1)} %collective-permute-done.6.refs_3_), channel_id=1, source_target_pairs={{0,4},{4,0},{8,12},{12,8},{16,20},{20,16},{24,28},{28,24},{1,5},{5... | collective-permute-start | bytes 786440 | tf_op jit(solution)/shard_map/ppermute | solution.py:416

commit v4 on v3

--- a/solution.py
+++ b/solution.py
@@ -12,7 +12,7 @@
 PANEL = 1024
 PIVOTS = 8
 ZEROS = 64
-EARLY = 0.375
+EARLY = 0.25
 MIB = 1 << 20
 
 SMEM = pl.BlockSpec(memory_space=pltpu.SMEM)

time: 64.1 us -> 63 us (0.983)
  waiting for transfers between devices: 8.67 us -> 10.2 us
  starting transfers between devices: 24.8 us -> 23.4 us
  Pallas kernels: 27.1 us -> 25.8 us
    ppermute x6, waiting for transfers between devices: 6.16 us -> 7.62 us  [along_tile(): return lax.ppermute(array, 'tile', [(t, t ^ k) for t in range(tile_count)])]
    pallas_call x1, Pallas kernels: 4.91 us -> 3.65 us  [local(): pl.pallas_call(functools.partial(fill_kernel, early), in_specs=[ANY], out...]
    ppermute x6, starting transfers between devices: 10.2 us -> 8.92 us  [along_tile(): return lax.ppermute(array, 'tile', [(t, t ^ k) for t in range(tile_count)])]
  transfers between devices with their start and end apart: 19 -> 19, of which waited for: 5 -> 6; matrix products, arithmetic and copies ran while one was open for 3% -> 3% of each run, Pallas kernels for 29% -> 27%
where the time goes in v4:
time: 63 us; the launch traced here: 62.6 us
  Pallas kernels  25.8 us (41%)
  starting transfers between devices  23.4 us (37%)
  waiting for transfers between devices  10.2 us (16%)
  local copies, waits for them, and re-layouts  1.67 us (3%)
  between operations  1.46 us (2%)
    pallas_call x1, Pallas kernels, local(): pl.pallas_call(functools.partial(factor_kernel, batch, block, ratio, row_...  9.97 us
    ppermute x6, starting transfers between devices, along_tile(): return lax.ppermute(array, 'tile', [(t, t ^ k) for t in range(tile_count)])  8.92 us
    ppermute x6, waiting for transfers between devices, along_tile(): return lax.ppermute(array, 'tile', [(t, t ^ k) for t in range(tile_count)])  7.62 us
    all_to_all x1, starting transfers between devices, local(): lax.all_to_all(main, both, 0, 0, tiled=True, axis_index_groups=teams)  7.01 us
    pallas_call x1, Pallas kernels, local(): pl.pallas_call(functools.partial(first_kernel, groups, block, group_size,...  5.76 us
    ppermute x3, starting transfers between devices, along_place(): return lax.ppermute(array, 'scen', pairs)  5.75 us
    pallas_call x1, Pallas kernels, local(): pl.pallas_call(functools.partial(fill_kernel, early), in_specs=[ANY], out...  3.65 us
    pallas_call x1, Pallas kernels, local(): pl.pallas_call(functools.partial(scatter_kernel, block), in_specs=[SMEM,...  3.49 us
  transfers between devices with their start and end apart: 19, of which 6 were waited for; matrix products, arithmetic and copies ran while one was open for 3% of the time, Pallas kernels for 27%

profile of v4, /device:TPU:0, one launch (start us, length us, event | category | flops | bytes accessed | tf_op | source)
XLA Modules:
  0.0 62.6 jit_solution(9502287571810450636)
XLA Ops:
  1.3 5.8 %shard_map.68 = (f32[16,128,128]{2,1,0:T(8,128)}, f32[208,128]{1,0:T(8,128)}, f32[208,128]{1,0:T(8,128)}, f32[208,128]{1,0:T(8,128)}, f32[208,128]{1,0:T(8,128)}) custom-call(s32[1,4]{1,0:T(1,128)} %touched_ref.1, s32[1]{0:T(128)S(6)} %copy.11.live_ref, f32[16,128]{1,0:T(8,128)} %bitcast.19, bf16[1024,1024]{1,0:T(8,128)(2,1)} %bitcast.22, ...), custom_call_target="tpu_custom_call" | custom-call | tf_op jit(solution)/shard_map/pallas_call | solution.py:391
  7.0 5.1 %collective-permute-start.2 = (f32[208,128]{1,0:T(8,128)}, f32[208,128]{1,0:T(8,128)S(1)}, u32[]{:S(2)}, u32[]{:S(2)}) collective-permute-start(f32[208,128]{1,0:T(8,128)} %get-tuple-element.32), channel_id=1, source_target_pairs={{0,24},{4,28},{8,16},{12,20},{16,8},{20,12},{24,0},{28,4},{1,25},{... | collective-permute-start | bytes 319496 | tf_op jit(solution)/shard_map/ppermute | solution.py:409
  12.2 0.0 collective-permute-start.1
  12.2 0.6 %collective-permute-start = (f32[208,128]{1,0:T(8,128)}, f32[208,128]{1,0:T(8,128)S(1)}, u32[]{:S(2)}, u32[]{:S(2)}) collective-permute-start(f32[208,128]{1,0:T(8,128)} %get-tuple-element.30), channel_id=1, source_target_pairs={{0,8},{4,12},{8,0},{12,4},{16,24},{20,28},{24,16},{28,20},{1,9},{5... | collective-permute-start | bytes 319496 | tf_op jit(solution)/shard_map/ppermute | solution.py:409
  12.8 7.0 %all-to-all-start = ((f32[16,128,128]{2,1,0:T(8,128)}), f32[16,128,128]{2,1,0:T(8,128)S(1)}, u32[]{:S(2)}, u32[]{:S(2)}) async-start(f32[16,128,128]{2,1,0:T(8,128)} %get-tuple-element.42), calls=%async_computation | async-start | bytes 2097152 | tf_op jit(solution)/shard_map/all_to_all | solution.py:443
  19.8 0.8 %slice_bitcast_fusion.3 = f32[1,128,128]{2,1,0:T(8,128)S(1)} fusion(f32[208,128]{1,0:T(8,128)} %get-tuple-element.29), kind=kLoop, calls=%fused_computation.5 | loop fusion | bytes 131072 | tf_op jit(solution)/shard_map/stack | solution.py:435
  20.7 0.8 %slice_bitcast_fusion.7 = f32[1,80,128]{2,1,0:T(8,128)S(1)} fusion(f32[208,128]{1,0:T(8,128)} %get-tuple-element.29), kind=kLoop, calls=%fused_computation.9 | loop fusion | bytes 81920 | tf_op jit(solution)/shard_map/stack | solution.py:425
  21.4 0.0 collective-permute-done.2
  21.5 0.0 collective-permute-done.1
  21.5 0.0 collective-permute-done
  21.5 2.0 %collective-permute-start.4 = (f32[4,80,128]{2,1,0:T(8,128)S(1)}, f32[4,80,128]{2,1,0:T(8,128)S(1)}, u32[]{:S(2)}, u32[]{:S(2)}) collective-permute-start(f32[4,80,128]{2,1,0:T(8,128)S(1)} %pad_maximum_fusion.1.refs_0_), channel_id=1, source_target_pairs={{0,1},{1,0},{2,3},{3,2},{4,5},{5,4},{6,7},{7,6},{8,9},{9,8},{10,11... | collective-permute-start | bytes 491528 | tf_op jit(solution)/shard_map/ppermute | solution.py:412
  23.5 1.5 %collective-permute-start.7 = (f32[4,80,128]{2,1,0:T(8,128)S(1)}, f32[4,80,128]{2,1,0:T(8,128)S(1)}, u32[]{:S(2)}, u32[]{:S(2)}) collective-permute-start(f32[4,80,128]{2,1,0:T(8,128)S(1)} %pad_maximum_fusion.1.refs_0_), channel_id=1, source_target_pairs={{0,2},{1,3},{2,0},{3,1},{4,6},{5,7},{6,4},{7,5},{8,10},{9,11},{10,... | collective-permute-start | bytes 491528 | tf_op jit(solution)/shard_map/ppermute | solution.py:412
  25.0 0.1 collective-permute-start.8
  25.1 0.0 collective-permute-start.9
  25.1 5.9 %collective-permute-done.4.after_ref.refs_1_ = f32[4,80,128]{2,1,0:T(8,128)S(1)} collective-permute-done((f32[4,80,128]{2,1,0:T(8,128)S(1)}, f32[4,80,128]{2,1,0:T(8,128)S(1)}, u32[]{:S(2)}, u32[]{:S(2)}) %collective-permute-start.4) | collective-permute-done | bytes 163872 | tf_op jit(solution)/shard_map/ppermute | solution.py:412
  31.0 0.0 collective-permute-start.10
  31.1 0.0 copy-start
  31.1 0.1 collective-permute-start.3
  31.1 3.6 %shard_map.69.refs_8_ = f32[2048,4096]{1,0:T(8,128)} custom-call(f32[4,80,128]{2,1,0:T(8,128)S(1)} %collective-permute-done.4.after_ref.refs_1_), custom_call_target="tpu_custom_call" | custom-call | bytes 8388608 | tf_op jit(solution)/shard_map/pallas_call | solution.py:426
  34.8 1.5 %collective-permute-done.7.refs_2_ = f32[4,80,128]{2,1,0:T(8,128)S(1)} collective-permute-done((f32[4,80,128]{2,1,0:T(8,128)S(1)}, f32[4,80,128]{2,1,0:T(8,128)S(1)}, u32[]{:S(2)}, u32[]{:S(2)}) %collective-permute-start.7) | collective-permute-done | bytes 163872 | tf_op jit(solution)/shard_map/ppermute | solution.py:412
  36.3 4.1 %collective-permute-start.5 = (f32[4,128,128]{2,1,0:T(8,128)S(1)}, f32[4,128,128]{2,1,0:T(8,128)S(1)}, u32[]{:S(2)}, u32[]{:S(2)}) collective-permute-start(f32[4,128,128]{2,1,0:T(8,128)S(1)} %pad_maximum_fusion.refs_0_), channel_id=1, source_target_pairs={{0,2},{1,3},{2,0},{3,1},{4,6},{5,7},{6,4},{7,5},{8,10},{9,11},{10,... | collective-permute-start | bytes 786440 | tf_op jit(solution)/shard_map/ppermute | solution.py:412
  40.4 0.0 collective-permute-done.8.refs_3_
  40.4 1.2 %collective-permute-start.6 = (f32[4,128,128]{2,1,0:T(8,128)S(1)}, f32[4,128,128]{2,1,0:T(8,128)S(1)}, u32[]{:S(2)}, u32[]{:S(2)}) collective-permute-start(f32[4,128,128]{2,1,0:T(8,128)S(1)} %pad_maximum_fusion.refs_0_), channel_id=1, source_target_pairs={{0,3},{1,2},{2,1},{3,0},{4,7},{5,6},{6,5},{7,4},{8,11},{9,10},{10,... | collective-permute-start | bytes 786440 | tf_op jit(solution)/shard_map/ppermute | solution.py:412
  41.6 0.0 collective-permute-done.9.refs_4_
  41.6 0.0 collective-permute-start.11
  41.6 0.0 collective-permute-done.10.refs_5_
  41.6 0.5 collective-permute-start.12
  42.1 0.9 %collective-permute-done.11.refs_6_ = f32[4,80,128]{2,1,0:T(8,128)S(1)} collective-permute-done((f32[4,80,128]{2,1,0:T(8,128)S(1)}, f32[4,80,128]{2,1,0:T(8,128)S(1)}, u32[]{:S(2)}, u32[]{:S(2)}) %collective-permute-start.11) | collective-permute-done | bytes 163872 | tf_op jit(solution)/shard_map/ppermute | solution.py:416
  43.0 0.2 collective-permute-done.12.refs_7_
  43.2 10.0 %shard_map.70 = (f32[1024,128]{1,0:T(8,128)S(1)}, f32[2048,4096]{1,0:T(8,128)}, s32[2,32]{1,0:T(2,128)S(1)}, s32[48]{0:T(128)S(1)}) custom-call(f32[4,80,128]{2,1,0:T(8,128)S(1)} %pad_maximum_fusion.1.refs_0_, f32[4,80,128]{2,1,0:T(8,128)S(1)} %collective-permute-done.4.after_ref.refs_1_, ...), custom_call_target="tpu_custom_call", output_to_operand_aliasing={{1}: (8, {})} | custom-call | tf_op jit(solution)/shard_map/pallas_call | solution.py:452
  53.2 0.0 collective-permute-done.3.refs_1_
  53.2 0.2 collective-permute-done.5.refs_2_
  53.4 0.0 collective-permute-done.6.refs_3_
  53.4 0.0 all-to-all-done.refs_0_
  53.4 0.2 collective-permute-start.17
  53.6 0.3 collective-permute-start.13
  53.9 0.2 collective-permute-start.14
  54.1 0.3 collective-permute-start.15
  54.4 0.2 collective-permute-start.16
  54.6 1.5 %collective-permute-done.17.refs_1_ = f32[16,128,128]{2,1,0:T(8,128)S(1)} collective-permute-done((f32[16,128,128]{2,1,0:T(8,128)S(1)}, f32[16,128,128]{2,1,0:T(8,128)S(1)}, u32[]{:S(2)}, u32[]{:S(2)}) %collective-permute-start.17) | collective-permute-done | bytes 1048608 | tf_op jit(solution)/shard_map/ppermute | solution.py:416
  56.1 0.0 copy-done
  56.1 3.5 %shard_map.71 = f32[2048,4096]{1,0:T(8,128)} custom-call(s32[2,32]{1,0:T(2,128)S(1)} %get-tuple-element.40.plan_ref, s32[48]{0:T(128)S(1)} %get-tuple-element.41.spot_ref, f32[16,128]{1,0:T(8,128)S(1)} %bitcast.20, f32[16,128,128]{2,1,0:T(8,128)S(1)} %all-to-all-done.refs_0_, ...), custom_call_target="tpu_custom_call", output_to_operand_aliasing={{}: (5, {})} | custom-call | tf_op jit(solution)/shard_map/pallas_call | solution.py:477
  59.6 0.0 collective-permute-done.13.refs_4_
  59.6 0.0 collective-permute-done.14.refs_5_
  59.6 0.0 collective-permute-done.15.refs_6_
  59.6 0.0 collective-permute-done.16.refs_7_
  59.6 2.9 %shard_map.72 = f32[512,1024]{1,0:T(8,128)} custom-call(s32[2,32]{1,0:T(2,128)S(1)} %get-tuple-element.40.plan_ref, f32[16,128]{1,0:T(8,128)S(1)} %bitcast.21, f32[1024,128]{1,0:T(8,128)S(1)} %get-tuple-element.47.inverse_ref, f32[4,128,128]{2,1,0:T(8,128)S(1)} %pad_maximum_fusion.refs_0_, f32[4,128,128]{2,1,0:T(8,128)S(1)} %collective-permute-done.3.refs_1_, ...), custom_call_target="tpu_custom_call" | custom-call | tf_op jit(solution)/shard_map/pallas_call | solution.py:488
  (8 shorter events, 0.1 us)
Async XLA Ops:
  7.0 14.4 %collective-permute-start.2 = (f32[208,128]{1,0:T(8,128)}, f32[208,128]{1,0:T(8,128)S(1)}, u32[]{:S(2)}, u32[]{:S(2)}) collective-permute-start(f32[208,128]{1,0:T(8,128)} %get-tuple-element.32), channel_id=1, source_target_pairs={{0,24},{4,28},{8,16},{12,20},{16,8},{20,12},{24,0},{28,4},{1,25},{... | collective-permute-start | bytes 319496 | tf_op jit(solution)/shard_map/ppermute | solution.py:409
  12.2 9.3 %collective-permute-start.1 = (f32[208,128]{1,0:T(8,128)}, f32[208,128]{1,0:T(8,128)S(1)}, u32[]{:S(2)}, u32[]{:S(2)}) collective-permute-start(f32[208,128]{1,0:T(8,128)} %get-tuple-element.31), channel_id=1, source_target_pairs={{0,16},{4,20},{8,24},{12,28},{16,0},{20,4},{24,8},{28,12},{1,17},{... | collective-permute-start | bytes 319496 | tf_op jit(solution)/shard_map/ppermute | solution.py:409
  12.2 9.3 %collective-permute-start = (f32[208,128]{1,0:T(8,128)}, f32[208,128]{1,0:T(8,128)S(1)}, u32[]{:S(2)}, u32[]{:S(2)}) collective-permute-start(f32[208,128]{1,0:T(8,128)} %get-tuple-element.30), channel_id=1, source_target_pairs={{0,8},{4,12},{8,0},{12,4},{16,24},{20,28},{24,16},{28,20},{1,9},{5... | collective-permute-start | bytes 319496 | tf_op jit(solution)/shard_map/ppermute | solution.py:409
  12.8 40.6 %all-to-all-start = ((f32[16,128,128]{2,1,0:T(8,128)}), f32[16,128,128]{2,1,0:T(8,128)S(1)}, u32[]{:S(2)}, u32[]{:S(2)}) async-start(f32[16,128,128]{2,1,0:T(8,128)} %get-tuple-element.42), calls=%async_computation | async-start | bytes 2097152 | tf_op jit(solution)/shard_map/all_to_all | solution.py:443
  21.5 9.5 %collective-permute-start.4 = (f32[4,80,128]{2,1,0:T(8,128)S(1)}, f32[4,80,128]{2,1,0:T(8,128)S(1)}, u32[]{:S(2)}, u32[]{:S(2)}) collective-permute-start(f32[4,80,128]{2,1,0:T(8,128)S(1)} %pad_maximum_fusion.1.refs_0_), channel_id=1, source_target_pairs={{0,1},{1,0},{2,3},{3,2},{4,5},{5,4},{6,7},{7,6},{8,9},{9,8},{10,11... | collective-permute-start | bytes 491528 | tf_op jit(solution)/shard_map/ppermute | solution.py:412
  23.5 12.8 %collective-permute-start.7 = (f32[4,80,128]{2,1,0:T(8,128)S(1)}, f32[4,80,128]{2,1,0:T(8,128)S(1)}, u32[]{:S(2)}, u32[]{:S(2)}) collective-permute-start(f32[4,80,128]{2,1,0:T(8,128)S(1)} %pad_maximum_fusion.1.refs_0_), channel_id=1, source_target_pairs={{0,2},{1,3},{2,0},{3,1},{4,6},{5,7},{6,4},{7,5},{8,10},{9,11},{10,... | collective-permute-start | bytes 491528 | tf_op jit(solution)/shard_map/ppermute | solution.py:412
  25.0 15.4 %collective-permute-start.8 = (f32[4,80,128]{2,1,0:T(8,128)S(1)}, f32[4,80,128]{2,1,0:T(8,128)S(1)}, u32[]{:S(2)}, u32[]{:S(2)}) collective-permute-start(f32[4,80,128]{2,1,0:T(8,128)S(1)} %pad_maximum_fusion.1.refs_0_), channel_id=1, source_target_pairs={{0,3},{1,2},{2,1},{3,0},{4,7},{5,6},{6,5},{7,4},{8,11},{9,10},{10,... | collective-permute-start | bytes 491528 | tf_op jit(solution)/shard_map/ppermute | solution.py:412
  25.1 16.5 %collective-permute-start.9 = (f32[4,80,128]{2,1,0:T(8,128)S(1)}, f32[4,80,128]{2,1,0:T(8,128)S(1)}, u32[]{:S(2)}, u32[]{:S(2)}) collective-permute-start(f32[4,80,128]{2,1,0:T(8,128)S(1)} %pad_maximum_fusion.1.refs_0_), channel_id=1, source_target_pairs={{0,4},{4,0},{8,12},{12,8},{16,20},{20,16},{24,28},{28,24},{1,5},{5... | collective-permute-start | bytes 491528 | tf_op jit(solution)/shard_map/ppermute | solution.py:416
  31.0 10.6 %collective-permute-start.10 = (f32[4,80,128]{2,1,0:T(8,128)S(1)}, f32[4,80,128]{2,1,0:T(8,128)S(1)}, u32[]{:S(2)}, u32[]{:S(2)}) collective-permute-start(f32[4,80,128]{2,1,0:T(8,128)S(1)} %collective-permute-done.4.after_ref.refs_1_), channel_id=1, source_target_pairs={{0,4},{4,0},{8,12},{12,8},{16,20},{20,16},{24,28},{28,24},{1,5},{5... | collective-permute-start | bytes 491528 | tf_op jit(solution)/shard_map/ppermute | solution.py:416
  31.1 25.0 %copy-start = (f32[2048]{0:T(1024)S(1)}, f32[2048]{0:T(1024)}, u32[]{:S(2)}) copy-start(f32[2048]{0:T(1024)} %param.9) | copy-start | bytes 24580
  31.1 22.2 %collective-permute-start.3 = (f32[4,128,128]{2,1,0:T(8,128)S(1)}, f32[4,128,128]{2,1,0:T(8,128)S(1)}, u32[]{:S(2)}, u32[]{:S(2)}) collective-permute-start(f32[4,128,128]{2,1,0:T(8,128)S(1)} %pad_maximum_fusion.refs_0_), channel_id=1, source_target_pairs={{0,1},{1,0},{2,3},{3,2},{4,5},{5,4},{6,7},{7,6},{8,9},{9,8},{10,11... | collective-permute-start | bytes 786440 | tf_op jit(solution)/shard_map/ppermute | solution.py:412
  36.3 17.1 %collective-permute-start.5 = (f32[4,128,128]{2,1,0:T(8,128)S(1)}, f32[4,128,128]{2,1,0:T(8,128)S(1)}, u32[]{:S(2)}, u32[]{:S(2)}) collective-permute-start(f32[4,128,128]{2,1,0:T(8,128)S(1)} %pad_maximum_fusion.refs_0_), channel_id=1, source_target_pairs={{0,2},{1,3},{2,0},{3,1},{4,6},{5,7},{6,4},{7,5},{8,10},{9,11},{10,... | collective-permute-start | bytes 786440 | tf_op jit(solution)/shard_map/ppermute | solution.py:412
  40.4 13.0 %collective-permute-start.6 = (f32[4,128,128]{2,1,0:T(8,128)S(1)}, f32[4,128,128]{2,1,0:T(8,128)S(1)}, u32[]{:S(2)}, u32[]{:S(2)}) collective-permute-start(f32[4,128,128]{2,1,0:T(8,128)S(1)} %pad_maximum_fusion.refs_0_), channel_id=1, source_target_pairs={{0,3},{1,2},{2,1},{3,0},{4,7},{5,6},{6,5},{7,4},{8,11},{9,10},{10,... | collective-permute-start | bytes 786440 | tf_op jit(solution)/shard_map/ppermute | solution.py:412
  41.6 1.4 %collective-permute-start.11 = (f32[4,80,128]{2,1,0:T(8,128)S(1)}, f32[4,80,128]{2,1,0:T(8,128)S(1)}, u32[]{:S(2)}, u32[]{:S(2)}) collective-permute-start(f32[4,80,128]{2,1,0:T(8,128)S(1)} %collective-permute-done.7.refs_2_), channel_id=1, source_target_pairs={{0,4},{4,0},{8,12},{12,8},{16,20},{20,16},{24,28},{28,24},{1,5},{5... | collective-permute-start | bytes 491528 | tf_op jit(solution)/shard_map/ppermute | solution.py:416
  41.6 1.6 %collective-permute-start.12 = (f32[4,80,128]{2,1,0:T(8,128)S(1)}, f32[4,80,128]{2,1,0:T(8,128)S(1)}, u32[]{:S(2)}, u32[]{:S(2)}) collective-permute-start(f32[4,80,128]{2,1,0:T(8,128)S(1)} %collective-permute-done.8.refs_3_), channel_id=1, source_target_pairs={{0,4},{4,0},{8,12},{12,8},{16,20},{20,16},{24,28},{28,24},{1,5},{5... | collective-permute-start | bytes 491528 | tf_op jit(solution)/shard_map/ppermute | solution.py:416
  53.4 2.7 %collective-permute-start.17 = (f32[16,128,128]{2,1,0:T(8,128)S(1)}, f32[16,128,128]{2,1,0:T(8,128)S(1)}, u32[]{:S(2)}, u32[]{:S(2)}) collective-permute-start(f32[16,128,128]{2,1,0:T(8,128)S(1)} %all-to-all-done.refs_0_), channel_id=1, source_target_pairs={{0,4},{4,0},{8,12},{12,8},{16,20},{20,16},{24,28},{28,24},{1,5},{5... | collective-permute-start | bytes 3145736 | tf_op jit(solution)/shard_map/ppermute | solution.py:416
  53.6 6.0 %collective-permute-start.13 = (f32[4,128,128]{2,1,0:T(8,128)S(1)}, f32[4,128,128]{2,1,0:T(8,128)S(1)}, u32[]{:S(2)}, u32[]{:S(2)}) collective-permute-start(f32[4,128,128]{2,1,0:T(8,128)S(1)} %pad_maximum_fusion.refs_0_), channel_id=1, source_target_pairs={{0,4},{4,0},{8,12},{12,8},{16,20},{20,16},{24,28},{28,24},{1,5},{5... | collective-permute-start | bytes 786440 | tf_op jit(solution)/shard_map/ppermute | solution.py:416
  53.9 5.7 %collective-permute-start.14 = (f32[4,128,128]{2,1,0:T(8,128)S(1)}, f32[4,128,128]{2,1,0:T(8,128)S(1)}, u32[]{:S(2)}, u32[]{:S(2)}) collective-permute-start(f32[4,128,128]{2,1,0:T(8,128)S(1)} %collective-permute-done.3.refs_1_), channel_id=1, source_target_pairs={{0,4},{4,0},{8,12},{12,8},{16,20},{20,16},{24,28},{28,24},{1,5},{5... | collective-permute-start | bytes 786440 | tf_op jit(solution)/shard_map/ppermute | solution.py:416
  54.1 5.5 %collective-permute-start.15 = (f32[4,128,128]{2,1,0:T(8,128)S(1)}, f32[4,128,128]{2,1,0:T(8,128)S(1)}, u32[]{:S(2)}, u32[]{:S(2)}) collective-permute-start(f32[4,128,128]{2,1,0:T(8,128)S(1)} %collective-permute-done.5.refs_2_), channel_id=1, source_target_pairs={{0,4},{4,0},{8,12},{12,8},{16,20},{20,16},{24,28},{28,24},{1,5},{5... | collective-permute-start | bytes 786440 | tf_op jit(solution)/shard_map/ppermute | solution.py:416
  54.4 5.2 %collective-permute-start.16 = (f32[4,128,128]{2,1,0:T(8,128)S(1)}, f32[4,128,128]{2,1,0:T(8,128)S(1)}, u32[]{:S(2)}, u32[]{:S(2)}) collective-permute-start(f32[4,128,128]{2,1,0:T(8,128)S(1)} %collective-permute-done.6.refs_3_), channel_id=1, source_target_pairs={{0,4},{4,0},{8,12},{12,8},{16,20},{20,16},{24,28},{28,24},{1,5},{5... | collective-permute-start | bytes 786440 | tf_op jit(solution)/shard_map/ppermute | solution.py:416
